TPU v7x, 512 devices: a whole 4x4x16 slice. The times are simulated.
512 devices in a mesh: gx: 32 (over z, core), gy: 16 (over x, y).
Axes of the slice: x: 4, y: 4, z: 16, core: 2. Of those that a mesh axis runs over, the one named last changes fastest.
Arguments:
- features: float32 [32, 16, 128, 256], P('gx', 'gy'), may hold values from -6 to 6
- offsets: float32 [32, 16, 3, 128], P('gx', 'gy'), may hold values from 0 to 1
- species: int32 [32, 16, 128], P('gx', 'gy'), may hold values from 0 to 63
- neighbours: int32 [32, 16, 128, 8], P('gx', 'gy'), may hold values from 0 to 65535, as said below
- edge_mask: int32 [32, 16, 128, 8], P('gx', 'gy'), may hold values 0 or 1
- wavevectors: int32 [3, 512], replicated, may hold values from -16 to 15, as said below
- value_weight: float32 [256, 256], replicated, may hold values from -0.375 to 0.375
- radial_weight: float32 [64, 256], replicated, may hold values from -3 to 3
- species_embed: float32 [64, 256], replicated, may hold values from -3 to 3
- mixing_weight: float32 [256, 256], replicated, may hold values from -0.375 to 0.375
- group_filter: float32 [32, 256, 256], P('gx'), may hold values from -0.375 to 0.375
Outputs:
- updated: float32 [32, 16, 128, 256], P('gx', 'gy')
Inputs may be any that keep to these rules, and one draw needn't show every extreme that they name: `neighbours`: every listed neighbour lies in a block whose first index differs from the atom's by at most one modulo 32 and whose second index differs by at most one modulo 16. `wavevectors`: the first component lies in -16 .. 15, the second in -8 .. 7, the third in -2 .. 2.
All inputs are finite; a program needn't handle non-finite values. No bound on the sum of `edge_mask` on one device may be relied on, other than what follows from the above.
Results may differ from a plain program's by a relative error of at most 0.0003.
Values sent between devices are 32-bit elements; how exact they have to be, the bound alone decides.
A program may use at most 64 MiB of HBM per device.

v0:
```python
import math

import jax
import jax.numpy as jnp
from jax import lax
from jax.sharding import PartitionSpec as P

FULL_TURN = 2.0 * math.pi
SMEARING = 0.01
RADIAL_REACH = 3.0
SOFTEN = 0.01
HIGHEST = lax.Precision.HIGHEST


def padded(cells, sides, width):
    for axis, dim in sides:
        count = lax.axis_size(axis)
        head = lax.slice_in_dim(cells, 0, width, axis=dim)
        tail = lax.slice_in_dim(cells, cells.shape[dim] - width, cells.shape[dim], axis=dim)
        cells = jnp.concatenate(
            [
                lax.ppermute(tail, axis, [(i, (i + 1) % count) for i in range(count)]),
                cells,
                lax.ppermute(head, axis, [((i + 1) % count, i) for i in range(count)]),
            ],
            axis=dim,
        )
    return cells


def cut_along(shard, dim, count):
    before, after = (shard.shape[:dim], shard.shape[dim + 1 :])
    return jnp.moveaxis(shard.reshape(*before, count, -1, *after), dim, 0)


def sum_at_owner(shard, axis, dim):
    count = lax.axis_size(axis)
    parts = lax.all_to_all(cut_along(shard, dim, count), axis, 0, 0, tiled=True)
    return jnp.sum(parts, axis=0)


def from_everyone(shard, axis):
    count = lax.axis_size(axis)
    return lax.all_to_all(
        jnp.broadcast_to(shard[None], (count, *shard.shape)), axis, 0, 0, tiled=True
    )


def of_everyone(shard, axis):
    everything = from_everyone(shard, axis)
    return jnp.sum(everything, axis=0)


def in_order(parts, dim):
    shape = list(parts.shape[1:])
    shape[dim] *= parts.shape[0]
    return jnp.moveaxis(parts, 0, dim).reshape(shape)


def gather_directly(shard, axis, dim):
    return in_order(from_everyone(shard, axis), dim)


def radial(distance, basis_count):
    centres = jnp.arange(basis_count, dtype=jnp.float32) * (RADIAL_REACH / (basis_count - 1))
    spread = 2.0 * RADIAL_REACH / (basis_count - 1)
    scaled = (distance[..., None] - centres) / spread
    return jnp.exp(-scaled * scaled)


def phase_table(
    vectors, lateral_block, transverse_block, offsets_block, lateral_span, transverse_span
):
    weights = vectors.astype(jnp.float32)
    lateral_whole = jnp.remainder(vectors[0] * lateral_block, lateral_span).astype(jnp.float32)
    transverse_whole = jnp.remainder(vectors[1] * transverse_block, transverse_span).astype(
        jnp.float32
    )
    fractions = (
        lateral_whole[None, :] + offsets_block[0][:, None] * weights[0][None, :]
    ) / lateral_span
    fractions = (
        fractions
        + (transverse_whole[None, :] + offsets_block[1][:, None] * weights[1][None, :])
        / transverse_span
    )
    fractions = fractions + offsets_block[2][:, None] * weights[2][None, :]
    return FULL_TURN * fractions


def damping(vectors, lateral_span, transverse_span):
    weights = vectors.astype(jnp.float32)
    lateral_wave = FULL_TURN * weights[0] / lateral_span
    transverse_wave = FULL_TURN * weights[1] / transverse_span
    vertical_wave = FULL_TURN * weights[2]
    return jnp.exp(
        -SMEARING
        * (
            lateral_wave * lateral_wave
            + transverse_wave * transverse_wave
            + vertical_wave * vertical_wave
        )
    )


def edge_messages(
    nearby_values,
    nearby_offsets,
    own_position,
    lateral_shift,
    transverse_shift,
    keep_mask,
    own_embed,
    nearby_embed,
    radial_weight,
    mixing_weight,
):
    lateral_gap = (
        lateral_shift.astype(jnp.float32) + nearby_offsets[..., 0] - own_position[:, None, 0]
    )
    transverse_gap = (
        transverse_shift.astype(jnp.float32) + nearby_offsets[..., 1] - own_position[:, None, 1]
    )
    vertical_gap = nearby_offsets[..., 2] - own_position[:, None, 2]
    distance = jnp.sqrt(
        lateral_gap * lateral_gap
        + transverse_gap * transverse_gap
        + vertical_gap * vertical_gap
        + SOFTEN
    )
    basis = radial(distance, radial_weight.shape[0])
    basis_rows = basis.reshape(-1, basis.shape[-1])
    before = jnp.dot(
        basis_rows, radial_weight, precision=HIGHEST, preferred_element_type=jnp.float32
    ).reshape(nearby_values.shape)
    hidden = jax.nn.silu(before + own_embed[:, None, :] + nearby_embed)
    filters = jnp.dot(
        hidden.reshape(-1, hidden.shape[-1]),
        mixing_weight,
        precision=HIGHEST,
        preferred_element_type=jnp.float32,
    ).reshape(nearby_values.shape)
    messages = filters * nearby_values * keep_mask.astype(jnp.float32)[..., None]
    return jnp.sum(messages, axis=1) / math.sqrt(nearby_values.shape[1])


def contract_atoms(table, feats):
    return lax.dot_general(
        table,
        feats,
        (((0,), (0,)), ((), ())),
        precision=HIGHEST,
        preferred_element_type=jnp.float32,
    )


def shards(
    features,
    offsets,
    species,
    neighbours,
    edge_mask,
    wavevectors,
    value_weight,
    radial_weight,
    species_embed,
    mixing_weight,
    group_filter,
):
    lateral_span = lax.axis_size("gx")
    transverse_span = lax.axis_size("gy")
    lateral_block = lax.axis_index("gx")
    transverse_block = lax.axis_index("gy")
    atom_count = features.shape[2]
    channel_count = features.shape[3]
    slot_count = neighbours.shape[3]
    mode_total = wavevectors.shape[1]
    kind_count = species_embed.shape[0]
    own_features = features[0, 0]
    own_offsets = offsets[0, 0]
    values = jnp.dot(
        own_features, value_weight, precision=HIGHEST, preferred_element_type=jnp.float32
    )
    carried = jnp.concatenate([own_offsets, species[0, 0].astype(jnp.float32)[None, :]], axis=0)
    nearby_values, nearby_carried = (
        padded(values[None, None], (("gx", 0), ("gy", 1)), 1),
        padded(carried[None, None], (("gx", 0), ("gy", 1)), 1),
    )
    flat_values = nearby_values.reshape(9 * atom_count, channel_count)
    flat_offsets = jnp.transpose(nearby_carried[:, :, :3, :], (0, 1, 3, 2)).reshape(
        9 * atom_count, 3
    )
    flat_species = nearby_carried[:, :, 3, :].reshape(9 * atom_count).astype(jnp.int32)
    one_hot = (flat_species[:, None] == jnp.arange(kind_count, dtype=jnp.int32)[None, :]).astype(
        jnp.float32
    )
    flat_embed = jnp.dot(
        one_hot, species_embed, precision=HIGHEST, preferred_element_type=jnp.float32
    )
    own_embed = flat_embed[4 * atom_count : 5 * atom_count]
    step_atoms = 64

    def edge_block(inputs):
        listed, keep_mask, own_position, own_rows = inputs
        source_block = listed // atom_count
        lateral_shift = (
            jnp.remainder(source_block // transverse_span - lateral_block + 1, lateral_span) - 1
        )
        transverse_shift = (
            jnp.remainder(source_block % transverse_span - transverse_block + 1, transverse_span)
            - 1
        )
        row_index = (
            (lateral_shift + 1) * 3 + (transverse_shift + 1)
        ) * atom_count + listed % atom_count
        return edge_messages(
            flat_values[row_index],
            flat_offsets[row_index],
            own_position,
            lateral_shift,
            transverse_shift,
            keep_mask,
            own_rows,
            flat_embed[row_index],
            radial_weight,
            mixing_weight,
        )

    nearby = lax.map(
        edge_block,
        (
            neighbours[0, 0].reshape(-1, step_atoms, slot_count),
            edge_mask[0, 0].reshape(-1, step_atoms, slot_count),
            jnp.transpose(own_offsets).reshape(-1, step_atoms, 3),
            own_embed.reshape(-1, step_atoms, channel_count),
        ),
    )
    nearby = nearby.reshape(atom_count, channel_count)
    group_rows = mode_total // lateral_span
    vectors = wavevectors
    angles = phase_table(
        vectors, lateral_block, transverse_block, own_offsets, lateral_span, transverse_span
    )
    partial_sum = sum_at_owner(
        jnp.concatenate(
            [
                contract_atoms(jnp.cos(angles), own_features),
                contract_atoms(jnp.sin(angles), own_features),
            ],
            axis=1,
        ),
        "gx",
        0,
    )
    owned = of_everyone(partial_sum, "gy")
    owned_vectors = lax.dynamic_slice_in_dim(wavevectors, lateral_block * group_rows, group_rows, 1)
    mixed = jnp.einsum(
        "mcf,fh->mch",
        owned.reshape(group_rows, 2, channel_count),
        group_filter[0],
        precision=HIGHEST,
        preferred_element_type=jnp.float32,
    )
    filtered = damping(owned_vectors, lateral_span, transverse_span)[:, None] * mixed.reshape(
        group_rows, 2 * channel_count
    )
    pieces = gather_directly(filtered, "gx", 0)
    vectors = wavevectors
    angles = phase_table(
        vectors, lateral_block, transverse_block, own_offsets, lateral_span, transverse_span
    )
    running = jnp.dot(
        jnp.cos(angles),
        pieces[:, :channel_count],
        precision=HIGHEST,
        preferred_element_type=jnp.float32,
    )
    distant = running + jnp.dot(
        jnp.sin(angles),
        pieces[:, channel_count:],
        precision=HIGHEST,
        preferred_element_type=jnp.float32,
    )
    scale = 1.0 / math.sqrt(atom_count * lateral_span * transverse_span * mode_total)
    return (nearby + distant * scale)[None, None]


def solution(mesh):
    placed = (
        P("gx", "gy", None, None),
        P("gx", "gy", None, None),
        P("gx", "gy", None),
        P("gx", "gy", None, None),
        P("gx", "gy", None, None),
        P(),
        P(),
        P(),
        P(),
        P(),
        P("gx", None, None),
    )
    return jax.shard_map(
        shards, mesh=mesh, in_specs=placed, out_specs=P("gx", "gy", None, None), check_vma=False
    )
```

profile of v0, /device:TPU:1, one launch (start us, length us, event | category | flops | bytes accessed | tf_op | source)
XLA Modules:
  0.0 188.2 jit_solution(14149331306734165970)
XLA Ops:
  0.0 0.7 convert_element_type.97
  1.5 0.8 fusion.98
  2.3 2.6 %fusion.46 = f32[512,256]{0,1:T(8,128)S(1)} fusion(f32[1,1,128,256]{3,2,1,0:T(8,128)} %param.13, f32[512]{0:T(512)S(1)} %bitcast.135, f32[128]{0:T(128)S(1)} %get-tuple-element.398, f32[512]{0:T(512)S(1)} %bitcast.139, f32[128]{0:T(128)S(1)} %get-tuple-element.399, f32[512]{0:T(512)S(1)} %bitcast.147, f32[512]{0:T(512)S(1)} %bitcast.131, ...), kind=kOutput, calls=%fused_computation.87 | convolution fusion | flops 201981952 | bytes 667136 | tf_op jit(solution)/shard_map/dot_general | solution.py:148
  4.9 2.5 %fusion.43 = f32[512,256]{0,1:T(8,128)S(1)} fusion(f32[1,1,128,256]{3,2,1,0:T(8,128)} %param.13, f32[512]{0:T(512)S(1)} %bitcast.136, f32[128]{0:T(128)S(1)} %get-tuple-element.398, f32[512]{0:T(512)S(1)} %bitcast.140, f32[128]{0:T(128)S(1)} %get-tuple-element.399, f32[512]{0:T(512)S(1)} %bitcast.148, f32[512]{0:T(512)S(1)} %bitcast.132, ...), kind=kOutput, calls=%fused_computation.86 | convolution fusion | flops 201981952 | bytes 667136 | tf_op jit(solution)/shard_map/dot_general | solution.py:148
  7.6 1.3 copy.47
  8.9 16.9 %all-to-all-start = ((f32[32,16,512]{2,1,0:T(8,128)}), f32[32,16,512]{2,1,0:T(8,128)S(1)}, u32[]{:S(2)}, u32[]{:S(2)}) async-start(f32[32,16,512]{2,1,0:T(8,128)} %bitcast.34), calls=%async_computation | async-start | bytes 2097152 | tf_op jit(solution)/shard_map/all_to_all | solution.py:38
  26.1 1.5 collective-permute-start
  27.9 1.3 collective-permute-start.5
  29.7 0.8 dynamic-slice_convert_fusion
  30.4 41.0 %collective-permute-done.1 = f32[1,1,4,128]{3,2,1,0:T(4,128)S(1)} collective-permute-done((f32[1,1,4,128]{3,2,1,0:T(4,128)S(1)}, f32[1,1,4,128]{3,2,1,0:T(4,128)S(1)}, u32[]{:S(2)}, u32[]{:S(2)}) %collective-permute-start.1) | collective-permute-done | bytes 2080 | tf_op jit(solution)/shard_map/ppermute | solution.py:24
  71.4 6.8 %collective-permute-start.3 = (f32[3,1,4,128]{3,2,1,0:T(4,128)S(1)}, f32[3,1,4,128]{3,2,1,0:T(4,128)S(1)}, u32[]{:S(2)}, u32[]{:S(2)}) collective-permute-start(f32[3,1,4,128]{3,2,1,0:T(4,128)S(1)} %pad_maximum_fusion.4), channel_id=1, source_target_pairs={{1,0},{2,1},{3,2},{4,3},{5,4},{6,5},{7,6},{8,7},{9,8},{10,9},{11,1... | collective-permute-start | bytes 18440 | tf_op jit(solution)/shard_map/ppermute | solution.py:24
  78.3 1.9 %collective-permute-start.2 = (f32[3,1,4,128]{3,2,1,0:T(4,128)S(1)}, f32[3,1,4,128]{3,2,1,0:T(4,128)S(1)}, u32[]{:S(2)}, u32[]{:S(2)}) collective-permute-start(f32[3,1,4,128]{3,2,1,0:T(4,128)S(1)} %pad_maximum_fusion.4), channel_id=1, source_target_pairs={{0,1},{1,2},{2,3},{3,4},{4,5},{5,6},{6,7},{7,8},{8,9},{9,10},{10,1... | collective-permute-start | bytes 18440 | tf_op jit(solution)/shard_map/ppermute | solution.py:22
  81.5 0.7 copy.44
  82.3 3.7 %collective-permute-done.2 = f32[3,1,4,128]{3,2,1,0:T(4,128)S(1)} collective-permute-done((f32[3,1,4,128]{3,2,1,0:T(4,128)S(1)}, f32[3,1,4,128]{3,2,1,0:T(4,128)S(1)}, u32[]{:S(2)}, u32[]{:S(2)}) %collective-permute-start.2) | collective-permute-done | bytes 6176 | tf_op jit(solution)/shard_map/ppermute | solution.py:22
  86.0 3.0 %collective-permute-start.7 = (f32[3,1,128,256]{3,2,1,0:T(8,128)S(1)}, f32[3,1,128,256]{3,2,1,0:T(8,128)S(1)}, u32[]{:S(2)}, u32[]{:S(2)}) collective-permute-start(f32[3,1,128,256]{3,2,1,0:T(8,128)S(1)} %pad_maximum_fusion.2), channel_id=1, source_target_pairs={{1,0},{2,1},{3,2},{4,3},{5,4},{6,5},{7,6},{8,7},{9,8},{10,9},{11,1... | collective-permute-start | bytes 1179656 | tf_op jit(solution)/shard_map/ppermute | solution.py:24
  89.0 2.3 %collective-permute-start.6 = (f32[3,1,128,256]{3,2,1,0:T(8,128)S(1)}, f32[3,1,128,256]{3,2,1,0:T(8,128)}, u32[]{:S(2)}, u32[]{:S(2)}) collective-permute-start(f32[3,1,128,256]{3,2,1,0:T(8,128)S(1)} %pad_maximum_fusion.2), channel_id=1, source_target_pairs={{0,1},{1,2},{2,3},{3,4},{4,5},{5,6},{6,7},{7,8},{8,9},{9,10},{10,1... | collective-permute-start | bytes 1179656 | tf_op jit(solution)/shard_map/ppermute | solution.py:22
  91.4 0.9 broadcast_in_dim.24
  92.3 5.8 %all-to-all-start.1 = ((f32[16,16,512]{2,1,0:T(8,128)}), f32[16,16,512]{2,1,0:T(8,128)}, u32[]{:S(2)}, u32[]{:S(2)}) async-start(f32[16,16,512]{2,1,0:T(8,128)} %broadcast_in_dim.24), calls=%async_computation.1 | async-start | bytes 1048576 | tf_op jit(solution)/shard_map/all_to_all | solution.py:44
  99.2 0.8 copy-done.9
  100.0 4.5 %collective-permute-done.6 = f32[3,1,128,256]{3,2,1,0:T(8,128)} collective-permute-done((f32[3,1,128,256]{3,2,1,0:T(8,128)S(1)}, f32[3,1,128,256]{3,2,1,0:T(8,128)}, u32[]{:S(2)}, u32[]{:S(2)}) %collective-permute-start.6) | collective-permute-done | bytes 393248 | tf_op jit(solution)/shard_map/ppermute | solution.py:22
  104.5 1.2 pad_maximum_fusion
  105.8 5.3 %all-to-all-done.1 = f32[16,16,512]{2,1,0:T(8,128)} async-done(((f32[16,16,512]{2,1,0:T(8,128)}), f32[16,16,512]{2,1,0:T(8,128)}, u32[]{:S(2)}, u32[]{:S(2)}) %all-to-all-start.1) | async-done | bytes 524320 | tf_op jit(solution)/shard_map/all_to_all | solution.py:44
  111.0 1.1 reduce_sum.35
  112.1 1.2 convolution_bitcast_fusion.1
  113.4 1.1 broadcast_in_dim.25
  114.5 12.2 %all-to-all-start.2 = ((f32[32,16,512]{2,1,0:T(8,128)}), f32[32,16,512]{2,1,0:T(8,128)}, u32[]{:S(2)}, u32[]{:S(2)}) async-start(f32[32,16,512]{2,1,0:T(8,128)} %broadcast_in_dim.25), calls=%async_computation.2 | async-start | bytes 2097152 | tf_op jit(solution)/shard_map/all_to_all | solution.py:44
  126.7 28.4 %while.15 = (s32[]{:T(128)}, f32[2,64,256]{2,1,0:T(8,128)}, s32[2,64,8]{1,0,2:T(2,128)S(1)}, s32[]{:T(128)}, s32[]{:T(128)}, /*index=5*/f32[1152,3]{1,0:T(8,128)...) while((s32[]{:T(128)}, f32[2,64,256]{2,1,0:T(8,128)}, ...), condition=%wide.region_2.3_spmd, body=%wide.region_0.2_spmd.sunk | while | flops 504703552 | bytes 10274961 | solution.py:229
  126.9 2.2 %gather_fusion = f32[512,256]{1,0:T(8,128)} fusion(f32[1152,256]{1,0:T(8,128)S(1)} %get-tuple-element.532, s32[1024]{0:T(1024)S(1)} %pad_clamp_fusion.2), kind=kCustom, calls=%fused_computation.2.clone.1 | custom fusion | bytes 1050624 | tf_op jit(solution)/shard_map/while/body/eval_jaxpr/gather | solution.py:217
  129.2 2.2 %gather_fusion.1 = f32[512,256]{1,0:T(8,128)} fusion(f32[1152,256]{1,0:T(8,128)S(1)} %get-tuple-element.530, s32[1024]{0:T(1024)S(1)} %pad_clamp_fusion.2), kind=kCustom, calls=%fused_computation.1.clone.1 | custom fusion | bytes 1050624 | tf_op jit(solution)/shard_map/while/body/eval_jaxpr/gather | solution.py:224
  132.0 1.0 gather_fusion.2
  133.0 1.0 fusion.129
  134.0 1.1 copy.74
  135.1 1.1 copy.75
  136.2 1.1 copy.76
  137.5 1.8 fusion.130
  139.3 0.7 fusion.131
  141.1 2.2 %gather_fusion = f32[512,256]{1,0:T(8,128)} fusion(f32[1152,256]{1,0:T(8,128)S(1)} %get-tuple-element.532, s32[1024]{0:T(1024)S(1)} %pad_clamp_fusion.2), kind=kCustom, calls=%fused_computation.2.clone.1 | custom fusion | bytes 1050624 | tf_op jit(solution)/shard_map/while/body/eval_jaxpr/gather | solution.py:217
  143.4 2.2 %gather_fusion.1 = f32[512,256]{1,0:T(8,128)} fusion(f32[1152,256]{1,0:T(8,128)S(1)} %get-tuple-element.530, s32[1024]{0:T(1024)S(1)} %pad_clamp_fusion.2), kind=kCustom, calls=%fused_computation.1.clone.1 | custom fusion | bytes 1050624 | tf_op jit(solution)/shard_map/while/body/eval_jaxpr/gather | solution.py:224
  146.2 1.0 gather_fusion.2
  147.2 1.0 fusion.129
  148.2 1.1 copy.74
  149.3 1.1 copy.75
  150.4 1.1 copy.76
  151.7 1.8 fusion.130
  153.5 0.7 fusion.131
  155.1 27.3 %all-to-all-done.2 = f32[32,16,512]{2,1,0:T(8,128)} async-done(((f32[32,16,512]{2,1,0:T(8,128)}), f32[32,16,512]{2,1,0:T(8,128)}, u32[]{:S(2)}, u32[]{:S(2)}) %all-to-all-start.2) | async-done | bytes 1048608 | tf_op jit(solution)/shard_map/all_to_all | solution.py:44
  182.4 2.5 %fusion.36 = f32[128,256]{1,0:T(8,128)S(1)} fusion(f32[512,512]{1,0:T(8,128)} %bitcast.37, f32[512]{0:T(512)} %bitcast.137, f32[128]{0:T(128)} %copy-done.23, f32[512]{0:T(512)} %bitcast.141, f32[128]{0:T(128)} %copy-done.24, f32[512]{0:T(512)} %bitcast.149, f32[512]{0:T(512)} %bitcast.133, f32[128]{0:T(128)} %copy-done.22, f32[512]{0:T(512)} %bitcast.145), kind=kOutput, calls=%fused_computation.78 | convolution fusion | flops 201981952 | bytes 667136 | tf_op jit(solution)/shard_map/dot_general | solution.py:272
  185.0 3.2 %fusion.33 = f32[1,1,128,256]{3,2,1,0:T(8,128)} fusion(f32[128,256]{1,0:T(8,128)} %bitcast.151, f32[128,256]{1,0:T(8,128)S(1)} %fusion.36, f32[512,512]{1,0:T(8,128)} %bitcast.37, f32[512]{0:T(512)} %bitcast.138, f32[128]{0:T(128)} %copy-done.23, f32[512]{0:T(512)} %bitcast.142, f32[128]{0:T(128)} %copy-done.24, f32[512]{0:T(512)} %bitcast.150, ...), kind=kOutput, calls=%fused_computation.72 | convolution fusion | flops 202080256 | bytes 929280 | tf_op jit(solution)/shard_map/dot_general | solution.py:278
  (132 shorter events, 7.9 us)
Async XLA Ops:
  0.0 27.6 %copy-start = (f32[256,256]{1,0:T(8,128)S(1)}, f32[256,256]{1,0:T(8,128)}, u32[]{:S(2)}) copy-start(f32[256,256]{1,0:T(8,128)} %param.19) | copy-start | bytes 786436
  0.8 4.1 %copy-start.17 = (f32[1,512]{1,0:T(1,128)}, f32[1,512]{1,0:T(1,128)S(1)}, u32[]{:S(2)}) copy-start(f32[1,512]{1,0:T(1,128)S(1)} %get-tuple-element.394) | copy-start | bytes 6148
  0.8 4.1 %copy-start.18 = (f32[1,512]{1,0:T(1,128)}, f32[1,512]{1,0:T(1,128)S(1)}, u32[]{:S(2)}) copy-start(f32[1,512]{1,0:T(1,128)S(1)} %get-tuple-element.395) | copy-start | bytes 6148
  0.8 4.1 %copy-start.19 = (f32[1,512]{1,0:T(1,128)}, f32[1,512]{1,0:T(1,128)S(1)}, u32[]{:S(2)}) copy-start(f32[1,512]{1,0:T(1,128)S(1)} %get-tuple-element.396) | copy-start | bytes 6148
  1.5 3.4 %copy-start.22 = (f32[128]{0:T(128)}, f32[128]{0:T(128)S(1)}, u32[]{:S(2)}) copy-start(f32[128]{0:T(128)S(1)} %get-tuple-element.397) | copy-start | bytes 1540
  1.5 3.4 %copy-start.23 = (f32[128]{0:T(128)}, f32[128]{0:T(128)S(1)}, u32[]{:S(2)}) copy-start(f32[128]{0:T(128)S(1)} %get-tuple-element.398) | copy-start | bytes 1540
  1.5 3.4 %copy-start.24 = (f32[128]{0:T(128)}, f32[128]{0:T(128)S(1)}, u32[]{:S(2)}) copy-start(f32[128]{0:T(128)S(1)} %get-tuple-element.399) | copy-start | bytes 1540
  2.3 2.6 %copy-start.20 = (f32[1,512]{1,0:T(1,128)}, f32[1,512]{1,0:T(1,128)S(1)}, u32[]{:S(2)}) copy-start(f32[1,512]{1,0:T(1,128)S(1)} %get-tuple-element.392) | copy-start | bytes 6148
  2.3 2.6 %copy-start.21 = (f32[1,512]{1,0:T(1,128)}, f32[1,512]{1,0:T(1,128)S(1)}, u32[]{:S(2)}) copy-start(f32[1,512]{1,0:T(1,128)S(1)} %get-tuple-element.393) | copy-start | bytes 6148
  8.9 16.9 %copy-start.13 = (f32[1,1,3,128]{3,1,2,0:T(1,128)S(1)}, f32[1,1,3,128]{3,1,2,0:T(1,128)}, u32[]{:S(2)}) copy-start(f32[1,1,3,128]{3,1,2,0:T(1,128)} %param.14) | copy-start | bytes 4612
  8.9 16.9 %copy-start.28 = (s32[1,1,128]{2,1,0:T(1,128)S(1)}, s32[1,1,128]{2,1,0:T(1,128)}, u32[]{:S(2)}) copy-start(s32[1,1,128]{2,1,0:T(1,128)} %param.15) | copy-start | bytes 1540
  8.9 18.7 %copy-start.10 = (f32[1,1,128,256]{3,2,1,0:T(8,128)S(1)}, f32[1,1,128,256]{3,2,1,0:T(8,128)}, u32[]{:S(2)}) copy-start(f32[1,1,128,256]{3,2,1,0:T(8,128)} %param.13) | copy-start | bytes 393220
  8.9 71.9 %copy-start.14 = (s32[1,1,128,8]{2,3,1,0:T(8,128)S(1)}, s32[1,1,128,8]{2,3,1,0:T(8,128)}, u32[]{:S(2)}) copy-start(s32[1,1,128,8]{2,3,1,0:T(8,128)} %param.16) | copy-start | bytes 12292
  8.9 72.7 %copy-start.15 = (s32[1,1,128,8]{2,3,1,0:T(8,128)S(1)}, s32[1,1,128,8]{2,3,1,0:T(8,128)}, u32[]{:S(2)}) copy-start(s32[1,1,128,8]{2,3,1,0:T(8,128)} %param.17) | copy-start | bytes 12292
  8.9 82.4 %all-to-all-start = ((f32[32,16,512]{2,1,0:T(8,128)}), f32[32,16,512]{2,1,0:T(8,128)S(1)}, u32[]{:S(2)}, u32[]{:S(2)}) async-start(f32[32,16,512]{2,1,0:T(8,128)} %bitcast.34), calls=%async_computation | async-start | bytes 2097152 | tf_op jit(solution)/shard_map/all_to_all | solution.py:38
  25.9 45.6 %collective-permute-start.1 = (f32[1,1,4,128]{3,2,1,0:T(4,128)S(1)}, f32[1,1,4,128]{3,2,1,0:T(4,128)S(1)}, u32[]{:S(2)}, u32[]{:S(2)}) collective-permute-start(f32[1,1,4,128]{3,2,1,0:T(4,128)S(1)} %maximum_bitcast_fusion), channel_id=1, source_target_pairs={{16,0},{32,16},{48,32},{64,48},{80,64},{96,80},{112,96},{128,112},... | collective-permute-start | bytes 6152 | tf_op jit(solution)/shard_map/ppermute | solution.py:24
  26.1 45.3 %collective-permute-start = (f32[1,1,4,128]{3,2,1,0:T(4,128)S(1)}, f32[1,1,4,128]{3,2,1,0:T(4,128)S(1)}, u32[]{:S(2)}, u32[]{:S(2)}) collective-permute-start(f32[1,1,4,128]{3,2,1,0:T(4,128)S(1)} %maximum_bitcast_fusion), channel_id=1, source_target_pairs={{0,16},{16,32},{32,48},{48,64},{64,80},{80,96},{96,112},{112,128},... | collective-permute-start | bytes 6152 | tf_op jit(solution)/shard_map/ppermute | solution.py:22
  27.9 58.1 %collective-permute-start.5 = (f32[1,1,128,256]{3,2,1,0:T(8,128)S(1)}, f32[1,1,128,256]{3,2,1,0:T(8,128)S(1)}, u32[]{:S(2)}, u32[]{:S(2)}) collective-permute-start(f32[1,1,128,256]{3,2,1,0:T(8,128)S(1)} %convolution_bitcast_fusion), channel_id=1, source_target_pairs={{16,0},{32,16},{48,32},{64,48},{80,64},{96,80},{112,96},{128,112},... | collective-permute-start | bytes 393224 | tf_op jit(solution)/shard_map/ppermute | solution.py:24
  29.3 56.7 %collective-permute-start.4 = (f32[1,1,128,256]{3,2,1,0:T(8,128)S(1)}, f32[1,1,128,256]{3,2,1,0:T(8,128)S(1)}, u32[]{:S(2)}, u32[]{:S(2)}) collective-permute-start(f32[1,1,128,256]{3,2,1,0:T(8,128)S(1)} %convolution_bitcast_fusion), channel_id=1, source_target_pairs={{0,16},{16,32},{32,48},{48,64},{64,80},{80,96},{96,112},{112,128},... | collective-permute-start | bytes 393224 | tf_op jit(solution)/shard_map/ppermute | solution.py:22
  71.4 10.8 %collective-permute-start.3 = (f32[3,1,4,128]{3,2,1,0:T(4,128)S(1)}, f32[3,1,4,128]{3,2,1,0:T(4,128)S(1)}, u32[]{:S(2)}, u32[]{:S(2)}) collective-permute-start(f32[3,1,4,128]{3,2,1,0:T(4,128)S(1)} %pad_maximum_fusion.4), channel_id=1, source_target_pairs={{1,0},{2,1},{3,2},{4,3},{5,4},{6,5},{7,6},{8,7},{9,8},{10,9},{11,1... | collective-permute-start | bytes 18440 | tf_op jit(solution)/shard_map/ppermute | solution.py:24
  78.3 7.7 %collective-permute-start.2 = (f32[3,1,4,128]{3,2,1,0:T(4,128)S(1)}, f32[3,1,4,128]{3,2,1,0:T(4,128)S(1)}, u32[]{:S(2)}, u32[]{:S(2)}) collective-permute-start(f32[3,1,4,128]{3,2,1,0:T(4,128)S(1)} %pad_maximum_fusion.4), channel_id=1, source_target_pairs={{0,1},{1,2},{2,3},{3,4},{4,5},{5,6},{6,7},{7,8},{8,9},{9,10},{10,1... | collective-permute-start | bytes 18440 | tf_op jit(solution)/shard_map/ppermute | solution.py:22
  86.0 6.3 %copy-start.5 = (f32[1,1,128,256]{3,2,1,0:T(8,128)}, f32[1,1,128,256]{3,2,1,0:T(8,128)S(1)}, u32[]{:S(2)}) copy-start(f32[1,1,128,256]{3,2,1,0:T(8,128)S(1)} %collective-permute-done.5) | copy-start | bytes 393220
  86.0 6.3 %copy-start.7 = (f32[1,1,128,256]{3,2,1,0:T(8,128)}, f32[1,1,128,256]{3,2,1,0:T(8,128)S(1)}, u32[]{:S(2)}) copy-start(f32[1,1,128,256]{3,2,1,0:T(8,128)S(1)} %collective-permute-done.4) | copy-start | bytes 393220
  86.0 13.2 %collective-permute-start.7 = (f32[3,1,128,256]{3,2,1,0:T(8,128)S(1)}, f32[3,1,128,256]{3,2,1,0:T(8,128)S(1)}, u32[]{:S(2)}, u32[]{:S(2)}) collective-permute-start(f32[3,1,128,256]{3,2,1,0:T(8,128)S(1)} %pad_maximum_fusion.2), channel_id=1, source_target_pairs={{1,0},{2,1},{3,2},{4,3},{5,4},{6,5},{7,6},{8,7},{9,8},{10,9},{11,1... | collective-permute-start | bytes 1179656 | tf_op jit(solution)/shard_map/ppermute | solution.py:24
  89.0 15.5 %collective-permute-start.6 = (f32[3,1,128,256]{3,2,1,0:T(8,128)S(1)}, f32[3,1,128,256]{3,2,1,0:T(8,128)}, u32[]{:S(2)}, u32[]{:S(2)}) collective-permute-start(f32[3,1,128,256]{3,2,1,0:T(8,128)S(1)} %pad_maximum_fusion.2), channel_id=1, source_target_pairs={{0,1},{1,2},{2,3},{3,4},{4,5},{5,6},{6,7},{7,8},{8,9},{9,10},{10,1... | collective-permute-start | bytes 1179656 | tf_op jit(solution)/shard_map/ppermute | solution.py:22
  91.4 7.0 %copy-start.11 = (f32[64,256]{1,0:T(8,128)S(1)}, f32[64,256]{1,0:T(8,128)}, u32[]{:S(2)}) copy-start(f32[64,256]{1,0:T(8,128)} %param.21) | copy-start | bytes 196612
  92.3 18.7 %all-to-all-start.1 = ((f32[16,16,512]{2,1,0:T(8,128)}), f32[16,16,512]{2,1,0:T(8,128)}, u32[]{:S(2)}, u32[]{:S(2)}) async-start(f32[16,16,512]{2,1,0:T(8,128)} %broadcast_in_dim.24), calls=%async_computation.1 | async-start | bytes 1048576 | tf_op jit(solution)/shard_map/all_to_all | solution.py:44
  98.5 6.0 %copy-start.6 = (f32[1,1,128,256]{3,2,1,0:T(8,128)S(1)}, f32[1,1,128,256]{3,2,1,0:T(8,128)}, u32[]{:S(2)}) copy-start(f32[1,1,128,256]{3,2,1,0:T(8,128)} %copy-done.5) | copy-start | bytes 393220
  98.5 6.0 %copy-start.8 = (f32[1,1,128,256]{3,2,1,0:T(8,128)S(1)}, f32[1,1,128,256]{3,2,1,0:T(8,128)}, u32[]{:S(2)}) copy-start(f32[1,1,128,256]{3,2,1,0:T(8,128)} %copy-done.7) | copy-start | bytes 393220
  99.2 14.1 %copy-start.16 = (f32[16]{0:T(128)S(1)}, f32[16]{0:T(128)}, u32[]{:S(2)}) copy-start(f32[16]{0:T(128)} %exponential_bitcast_fusion) | copy-start | bytes 196
  99.2 0.8 copy-start.9
  114.5 68.0 %all-to-all-start.2 = ((f32[32,16,512]{2,1,0:T(8,128)}), f32[32,16,512]{2,1,0:T(8,128)}, u32[]{:S(2)}, u32[]{:S(2)}) async-start(f32[32,16,512]{2,1,0:T(8,128)} %broadcast_in_dim.25), calls=%async_computation.2 | async-start | bytes 2097152 | tf_op jit(solution)/shard_map/all_to_all | solution.py:44
  126.7 4.7 %copy-start.2 = (f32[2,64,256]{2,1,0:T(8,128)}, f32[2,64,256]{2,1,0:T(8,128)S(1)}, u32[]{:S(2)}) copy-start(f32[2,64,256]{2,1,0:T(8,128)S(1)} %get-tuple-element.529) | copy-start | bytes 393220 | tf_op jit(solution)/shard_map/while
  133.0 4.3 %copy-start.12 = (f32[2,64,3]{1,0,2:T(2,128)S(1)}, f32[2,64,3]{1,0,2:T(2,128)}, u32[]{:S(2)}) copy-start(f32[2,64,3]{1,0,2:T(2,128)} %get-tuple-element.527) | copy-start | bytes 4612 | tf_op jit(solution)/shard_map/while
  134.0 5.3 %copy-start.4 = (s32[2,64,8]{2,1,0:T(8,128)S(1)}, s32[2,64,8]{2,1,0:T(8,128)}, u32[]{:S(2)}) copy-start(s32[2,64,8]{2,1,0:T(8,128)} %get-tuple-element.533) | copy-start | bytes 12292 | tf_op jit(solution)/shard_map/while
  137.5 1.8 copy-start.1
  137.5 1.8 copy-start.25
  139.3 0.9 copy-start.26
  139.3 1.6 copy-start.3
  140.2 0.7 copy-start.27
  140.9 4.7 %copy-start.2 = (f32[2,64,256]{2,1,0:T(8,128)}, f32[2,64,256]{2,1,0:T(8,128)S(1)}, u32[]{:S(2)}) copy-start(f32[2,64,256]{2,1,0:T(8,128)S(1)} %get-tuple-element.529) | copy-start | bytes 393220 | tf_op jit(solution)/shard_map/while
  147.2 4.3 %copy-start.12 = (f32[2,64,3]{1,0,2:T(2,128)S(1)}, f32[2,64,3]{1,0,2:T(2,128)}, u32[]{:S(2)}) copy-start(f32[2,64,3]{1,0,2:T(2,128)} %get-tuple-element.527) | copy-start | bytes 4612 | tf_op jit(solution)/shard_map/while
  148.2 5.3 %copy-start.4 = (s32[2,64,8]{2,1,0:T(8,128)S(1)}, s32[2,64,8]{2,1,0:T(8,128)}, u32[]{:S(2)}) copy-start(s32[2,64,8]{2,1,0:T(8,128)} %get-tuple-element.533) | copy-start | bytes 12292 | tf_op jit(solution)/shard_map/while
  151.7 1.8 copy-start.1
  151.7 1.8 copy-start.25
  153.5 0.9 copy-start.26
  153.5 1.6 copy-start.3
  154.4 0.7 copy-start.27
where the time goes:
time: 189 us; the launch traced here: 188 us
  waiting for transfers between devices  81.8 us (43%)
  starting transfers between devices  52.5 us (28%)
  local copies, waits for them, and re-layouts  28.3 us (15%)
  matrix products  18 us (10%)
  other arithmetic  6.77 us (4%)
    ppermute x4, waiting for transfers between devices, padded(): lax.ppermute(head, axis, [((i + 1) % count, i) for i in range(count)])  41 us
    all_to_all x2, waiting for transfers between devices, from_everyone(): lax.all_to_all(jnp.broadcast_to(shard[None], (count, *shard.shape)), axis...  32.6 us
    all_to_all x2, starting transfers between devices, from_everyone(): lax.all_to_all(jnp.broadcast_to(shard[None], (count, *shard.shape)), axis...  18 us
    all_to_all x1, starting transfers between devices, sum_at_owner(): parts = lax.all_to_all(cut_along(shard, dim, count), axis, 0, 0, tiled=True)  16.9 us
    ppermute x4, starting transfers between devices, padded(): lax.ppermute(head, axis, [((i + 1) % count, i) for i in range(count)])  11.4 us
    ppermute x4, waiting for transfers between devices, padded(): lax.ppermute(tail, axis, [(i, (i + 1) % count) for i in range(count)])  8.22 us
    while x38, local copies, waits for them, and re-layouts  8.19 us
    ppermute x4, starting transfers between devices, padded(): lax.ppermute(tail, axis, [(i, (i + 1) % count) for i in range(count)])  6.13 us
  transfers between devices with their start and end apart: 11, of which 5 were waited for; matrix products, arithmetic and copies ran while one was open for 17% of the time, Pallas kernels for 0%

commit v1 on v0

v1 whole, which is shorter than its diff:
```python
import math

import jax
import jax.numpy as jnp
from jax import lax
from jax.experimental import pallas as pl
from jax.experimental.pallas import tpu as pltpu
from jax.sharding import PartitionSpec as P

MESH = pl.DeviceIdType.MESH
F32 = jnp.float32
BF16 = jnp.bfloat16

GX = 32
GY = 16
NZ = 16
ATOMS = 128
CH = 256
MODES = 512
SLOTS = 8
RADIAL = 64
SCALE = 1.0 / math.sqrt(33554432)
TURN = 2.0 * math.pi

COS_TERMS = [(-1.0) ** n * TURN ** (2 * n) / math.factorial(2 * n) for n in range(7)]
SIN_TERMS = [(-1.0) ** n * TURN ** (2 * n + 1) / math.factorial(2 * n + 1) for n in range(7)]


def halves(x):
    hi = x.astype(BF16)
    return hi, (x - hi.astype(F32)).astype(BF16)


def mm(a, b):
    return jnp.dot(a, b, preferred_element_type=F32)


def mm3(a_hi, a_lo, b_hi, b_lo):
    return mm(a_hi, b_hi) + (mm(a_hi, b_lo) + mm(a_lo, b_hi))


def cos_sin(turns):
    q = jnp.floor(turns * 2.0 + 0.5)
    r = turns - q * 0.5
    h = q * 0.5
    sign = 1.0 - 4.0 * (h - jnp.floor(h))
    y = r * r
    c = jnp.full_like(y, COS_TERMS[6])
    s = jnp.full_like(y, SIN_TERMS[6])
    for n in range(5, -1, -1):
        c = c * y + COS_TERMS[n]
        s = s * y + SIN_TERMS[n]
    return c * sign, s * (r * sign)


def remote(src, dst, send, recv, gx, gy):
    return pltpu.make_async_remote_copy(
        src_ref=src, dst_ref=dst, send_sem=send, recv_sem=recv, device_id=(gx, gy), device_id_type=MESH
    )


def kernel(
    feat, offs, spec, neigh, mask, wv, wv_s, vw, radw, emb, mixw, gf,
    out,
    feat2, carry2, halo, tf, t_hi, t_lo, tt_hi, tt_lo, ncol, wpad,
    part, got1, sums, got2, rows16, filt1, filt2, filt3, rh_hi, rh_lo, lpeer, lgot,
    nb_pad, dist, spj, rowid, onehot, bh, bl, filt, wcat, mix_hi, mix_lo, vb,
    s_feat, r_feat, s_halo, r_halo, s_rs1, r_rs1, s_rs2, r_rs2, s_ag1, r_ag1, s_ag2, r_ag2, s_fin, r_fin,
):
    gx = lax.axis_index("gx")
    gy = lax.axis_index("gy")
    c = lax.rem(gx, 2)
    z = gx // 2
    px = gy // 4
    py = lax.rem(gy, 4)
    peer = gx + 1 - 2 * c
    other = lax.rem(gx + 31 + 2 * c, GX)

    def plane(k):
        return lax.rem(px + k // 4, 4) * 4 + lax.rem(py + k % 4, 4)

    def column(k):
        return 2 * lax.rem(z + k, NZ) + c

    barrier = pltpu.get_barrier_semaphore()
    greeted = [(gx, plane(k)) for k in range(1, 16)]
    greeted += [(column(k), gy) for k in range(1, 16)]
    greeted += [(peer, gy), (other, gy)]
    up = lax.rem(gy + 1, GY)
    down = lax.rem(gy + GY - 1, GY)
    for device in greeted:
        pl.semaphore_signal(barrier, inc=1, device_id=device, device_id_type=MESH)

    f_hi, f_lo = halves(feat[0, 0])
    vw_hi, vw_lo = halves(vw[...])
    halo[4, 0:CH, :] = jnp.transpose(mm3(f_hi, f_lo, vw_hi, vw_lo))
    halo[4, CH:CH + 8, :] = jnp.zeros((8, ATOMS), F32)
    halo[4, CH:CH + 3, :] = offs[0, 0]
    halo[4, CH + 3:CH + 4, :] = spec[0].astype(F32)

    wpad[...] = jnp.zeros(wpad.shape, F32)
    wpad[0:3, :] = wv[...].astype(F32)
    r = lax.broadcasted_iota(jnp.int32, (256, MODES), 0)
    m = lax.broadcasted_iota(jnp.int32, (256, MODES), 1)
    pick = jnp.where((2 * (r & 15) + c) * 16 + (r >> 4) == m, 1.0, 0.0).astype(BF16)
    ncol[...] = lax.dot_general(
        pick, wpad[...].astype(BF16), (((1,), (1,)), ((), ())), preferred_element_type=F32
    )

    pl.semaphore_wait(barrier, len(greeted))

    sends = []

    def start(*a):
        copy = remote(*a)
        copy.start()
        sends.append(copy)

    def arrived(dst, sem):
        remote(dst, dst, s_fin.at[0], sem, peer, gy).wait_recv()

    start(halo.at[4, pl.ds(CH, 8)], carry2, s_feat.at[0], r_feat.at[0], peer, gy)
    start(feat.at[0, 0], feat2, s_feat.at[1], r_feat.at[1], peer, gy)
    start(halo.at[4], halo.at[3], s_halo.at[0], r_halo.at[0], gx, up)
    start(halo.at[4], halo.at[5], s_halo.at[1], r_halo.at[1], gx, down)
    start(halo.at[4], halo.at[(2 - 2 * c) * 3 + 1], s_halo.at[6], r_halo.at[6], other, gy)
    start(halo.at[4], halo.at[2 * c * 3 + 1], s_halo.at[3], r_halo.at[3], peer, gy)

    def table(block, positions, lane):
        def step(i, carry):
            n = ncol[pl.ds(pl.multiple_of(i * 64, 64), 64), :]
            n0, n1, n2 = n[:, 0:1], n[:, 1:2], n[:, 2:3]
            w0 = (n0.astype(jnp.int32) * block & 31).astype(F32)
            w1 = (n1.astype(jnp.int32) * gy & 15).astype(F32)
            turns = (w0 + n0 * positions[0:1, :]) * (1.0 / 32)
            turns = turns + (w1 + n1 * positions[1:2, :]) * (1.0 / 16)
            turns = turns + n2 * positions[2:3, :]
            cosine, sine = cos_sin(turns)
            for at, value in ((0, cosine), (64, sine)):
                tf[i, at:at + 64, lane:lane + ATOMS] = value
                hi, lo = halves(value)
                t_hi[i, at:at + 64, lane:lane + ATOMS] = hi
                t_lo[i, at:at + 64, lane:lane + ATOMS] = lo
            return carry

        lax.fori_loop(0, 4, step, 0)

    table(gx, halo[4, CH:CH + 8, :], 0)
    arrived(carry2, r_feat.at[0])
    table(peer, carry2[...], ATOMS)
    arrived(feat2, r_feat.at[1])
    g_hi, g_lo = halves(feat2[...])
    both_hi = jnp.concatenate([f_hi, g_hi], axis=0)
    both_lo = jnp.concatenate([f_lo, g_lo], axis=0)
    for dx in (2, 1, 3, 0):
        xx = lax.rem(px + dx, 4)
        a_hi, a_lo = t_hi[xx], t_lo[xx]
        p = mm3(a_hi, a_lo, both_hi, both_lo)
        for y in range(4):
            part[xx * 4 + y, :, 0:CH] = p[16 * y:16 * y + 16]
            part[xx * 4 + y, :, CH:2 * CH] = p[64 + 16 * y:64 + 16 * y + 16]
        for dy in (2, 1, 3, 0):
            k = dx * 4 + dy
            if k:
                start(part.at[plane(k)], got1.at[k], s_rs1.at[k], r_rs1.at[k], gx, plane(k))

    for t, slot in ((0, 3), (2, 5)):
        arrived(halo.at[slot], r_halo.at[t // 2])
        start(halo.at[slot], halo.at[(2 - 2 * c) * 3 + t], s_halo.at[5 + t], r_halo.at[5 + t], other, gy)
        start(halo.at[slot], halo.at[2 * c * 3 + t], s_halo.at[2 + t], r_halo.at[2 + t], peer, gy)

    for i in range(4):
        hi, lo = halves(jnp.transpose(tf[i]))
        tt_hi[:, 128 * i:128 * i + 128] = hi
        tt_lo[:, 128 * i:128 * i + 128] = lo
    wt = jnp.transpose(jnp.concatenate([radw[...], emb[...]], axis=0))
    hi, lo = halves(wt)
    wcat[:, 0:128] = hi
    wcat[:, 128:256] = lo
    hi, lo = halves(jnp.transpose(mixw[...]))
    mix_hi[...] = hi
    mix_lo[...] = lo
    nb_pad[...] = jnp.zeros(nb_pad.shape, jnp.int32)
    nb_pad[:, 0:SLOTS] = jnp.where(mask[0, 0] > 0, neigh[0, 0], -1)
    listed = jnp.transpose(nb_pad[...])[0:SLOTS]

    for t in range(3):
        arrived(halo.at[(2 - 2 * c) * 3 + t], r_halo.at[2 + t])
        arrived(halo.at[2 * c * 3 + t], r_halo.at[5 + t])

    source = listed >> 7
    atom = listed & 127
    s = (((source >> 4) - gx + 1) & 31) - 1
    t = (((source & 15) - gy + 1) & 15) - 1
    near = (s + 1) * 3 + (t + 1)
    found = [jnp.zeros((SLOTS, ATOMS), F32) for _ in range(4)]
    for j in range(9):
        for i in range(4):
            row = jnp.broadcast_to(halo[j, CH + i:CH + i + 1, :], (SLOTS, ATOMS))
            taken = jnp.take_along_axis(row, atom, axis=1)
            found[i] = jnp.where(near == j, taken, found[i])
    own = halo[4, CH:CH + 8, :]
    gap0 = (s.astype(F32) + found[0]) - own[0:1, :]
    gap1 = (t.astype(F32) + found[1]) - own[1:2, :]
    gap2 = found[2] - own[2:3, :]
    dist[...] = jnp.sqrt(gap0 * gap0 + gap1 * gap1 + gap2 * gap2 + 0.01)
    spj[...] = found[3]
    rowid[...] = jnp.where(listed < 0, -1, near * ATOMS + atom)
    own_kind = own[3:4, :]

    def slot_step(e, carry):
        lanes = pl.ds(pl.multiple_of(e * ATOMS, ATOMS), ATOMS)
        k = lax.broadcasted_iota(jnp.int32, (RADIAL, ATOMS), 0).astype(F32)
        scaled = (dist[pl.ds(e, 1), :] - k * (3.0 / 63)) / (6.0 / 63)
        hi, lo = halves(jnp.exp(-scaled * scaled))
        kinds = jnp.where(k == spj[pl.ds(e, 1), :], 1.0, 0.0) + jnp.where(k == own_kind, 1.0, 0.0)
        kinds = kinds.astype(BF16)
        bh[0:64, lanes] = hi
        bh[64:128, lanes] = kinds
        bh[128:192, lanes] = hi
        bh[192:256, lanes] = kinds
        bl[:, lanes] = lo
        place = rowid[pl.ds(e, 1), :]
        at = lax.broadcasted_iota(jnp.int32, (ATOMS, ATOMS), 0)
        for j in range(9):
            hit = jnp.where(at == place - ATOMS * j, 1.0, 0.0)
            onehot[ATOMS * j:ATOMS * j + ATOMS, lanes] = hit.astype(BF16)
        return carry

    lax.fori_loop(0, SLOTS, slot_step, 0)

    def filter_step(e, carry):
        lanes = pl.ds(pl.multiple_of(e * 256, 256), 256)
        before = mm(wcat[...], bh[:, lanes]) + mm(wcat[:, 0:64], bl[:, lanes])
        hi, lo = halves(before / (1.0 + jnp.exp(-before)))
        filt[:, lanes] = mm3(mix_hi[...], mix_lo[...], hi, lo)
        return carry

    lax.fori_loop(0, 4, filter_step, 0)

    total = part[gy]
    for k in range(1, 16):
        arrived(got1.at[k], r_rs1.at[k])
        total = total + got1[k]
    for k in range(NZ):
        sums[k] = total[k:k + 1, :]
    for k in range(1, 16):
        dz = lax.rem(z + k, NZ)
        start(sums.at[dz], got2.at[k], s_rs2.at[k], r_rs2.at[k], 2 * dz + c, gy)

    gf_hi, gf_lo = halves(gf[0])
    mode = gx * 16 + gy
    wave0 = jnp.full((1, CH), wv_s[0, mode], jnp.int32).astype(F32) * (TURN / 32)
    wave1 = jnp.full((1, CH), wv_s[1, mode], jnp.int32).astype(F32) * (TURN / 16)
    wave2 = jnp.full((1, CH), wv_s[2, mode], jnp.int32).astype(F32) * TURN
    damp = jnp.exp(-0.01 * (wave0 * wave0 + wave1 * wave1 + wave2 * wave2)) * SCALE
    rows16[...] = jnp.zeros(rows16.shape, F32)

    total = sums[z]
    for k in range(1, 16):
        arrived(got2.at[k], r_rs2.at[k])
        total = total + got2[k]
    rows16[0:1, :] = total[:, 0:CH]
    rows16[1:2, :] = total[:, CH:2 * CH]
    a_hi, a_lo = halves(rows16[...])
    mixed = mm3(a_hi, a_lo, gf_hi, gf_lo)
    filt1[z, :, 0:CH] = mixed[0:1, :] * damp
    filt1[z, :, CH:2 * CH] = mixed[1:2, :] * damp
    for k in range(1, 16):
        dz = lax.rem(z + k, NZ)
        start(filt1.at[z], filt1.at[z], s_ag1.at[k], r_ag1.at[k], 2 * dz + c, gy)
    for k in range(1, 16):
        arrived(filt1.at[lax.rem(z + NZ - k, NZ)], r_ag1.at[k])
    for k in range(NZ):
        filt2[k:k + 1, :] = filt1[k]
    for k in (10, 9, 11, 6, 14, 8, 2, 5, 7, 13, 15, 4, 12, 1, 3):
        start(filt2, filt3.at[gy], s_ag2.at[k], r_ag2.at[k], gx, plane(k))
    filt3[gy] = filt2[...]

    for j in range(9):
        hi, lo = halves(halo[j, 0:CH, :])
        vb[0:CH, ATOMS * j:ATOMS * j + ATOMS] = hi
        vb[CH:2 * CH, ATOMS * j:ATOMS * j + ATOMS] = lo

    def gather_step(e, acc):
        lanes = pl.ds(pl.multiple_of(e * 256, 256), 256)
        g = mm(vb[...], onehot[:, lanes])
        msg = (g[0:CH] + g[CH:2 * CH]) * filt[:, lanes]
        return acc + (msg[:, 0:ATOMS] + msg[:, ATOMS:2 * ATOMS])

    short = lax.fori_loop(0, 4, gather_step, jnp.zeros((CH, ATOMS), F32))
    out[0, 0] = jnp.transpose(short) * (1.0 / math.sqrt(SLOTS))

    for k in range(1, 16):
        arrived(filt3.at[lax.rem(px + 4 - k // 4, 4) * 4 + lax.rem(py + 4 - k % 4, 4)], r_ag2.at[k])
    for i in range(4):
        for y in range(4):
            hi, lo = halves(filt3[4 * i + y])
            for at, lane in ((0, 0), (64, CH)):
                row = 128 * i + at + 16 * y
                rh_hi[row:row + 16, :] = hi[:, lane:lane + CH]
                rh_lo[row:row + 16, :] = lo[:, lane:lane + CH]
    lpeer[...] = mm3(tt_hi[ATOMS:], tt_lo[ATOMS:], rh_hi[...], rh_lo[...])
    start(lpeer, lgot, s_fin.at[0], r_fin.at[0], peer, gy)
    mine = mm3(tt_hi[0:ATOMS], tt_lo[0:ATOMS], rh_hi[...], rh_lo[...])
    base = out[0, 0] + mine
    arrived(lgot, r_fin.at[0])
    out[0, 0] = base + lgot[...]
    for copy in sends:
        copy.wait_send()


def shards(features, offsets, species, neighbours, edge_mask, wavevectors, vw, radw, emb, mixw, gf):
    vmem = pl.BlockSpec(memory_space=pltpu.VMEM)
    smem = pl.BlockSpec(memory_space=pltpu.SMEM)
    dma = pltpu.SemaphoreType.DMA
    scratch = [
        pltpu.VMEM((ATOMS, CH), F32),
        pltpu.VMEM((8, ATOMS), F32),
        pltpu.VMEM((9, CH + 8, ATOMS), F32),
        pltpu.VMEM((4, 128, 2 * ATOMS), F32),
        pltpu.VMEM((4, 128, 2 * ATOMS), BF16),
        pltpu.VMEM((4, 128, 2 * ATOMS), BF16),
        pltpu.VMEM((2 * ATOMS, 512), BF16),
        pltpu.VMEM((2 * ATOMS, 512), BF16),
        pltpu.VMEM((256, 128), F32),
        pltpu.VMEM((128, MODES), F32),
        pltpu.VMEM((GY, NZ, 2 * CH), F32),
        pltpu.VMEM((GY, NZ, 2 * CH), F32),
        pltpu.VMEM((NZ, 1, 2 * CH), F32),
        pltpu.VMEM((NZ, 1, 2 * CH), F32),
        pltpu.VMEM((16, CH), F32),
        pltpu.VMEM((NZ, 1, 2 * CH), F32),
        pltpu.VMEM((NZ, 2 * CH), F32),
        pltpu.VMEM((GY, NZ, 2 * CH), F32),
        pltpu.VMEM((512, CH), BF16),
        pltpu.VMEM((512, CH), BF16),
        pltpu.VMEM((ATOMS, CH), F32),
        pltpu.VMEM((ATOMS, CH), F32),
        pltpu.VMEM((ATOMS, ATOMS), jnp.int32),
        pltpu.VMEM((SLOTS, ATOMS), F32),
        pltpu.VMEM((SLOTS, ATOMS), F32),
        pltpu.VMEM((SLOTS, ATOMS), jnp.int32),
        pltpu.VMEM((9 * ATOMS, SLOTS * ATOMS), BF16),
        pltpu.VMEM((256, SLOTS * ATOMS), BF16),
        pltpu.VMEM((64, SLOTS * ATOMS), BF16),
        pltpu.VMEM((CH, SLOTS * ATOMS), F32),
        pltpu.VMEM((CH, 256), BF16),
        pltpu.VMEM((CH, CH), BF16),
        pltpu.VMEM((CH, CH), BF16),
        pltpu.VMEM((2 * CH, 9 * ATOMS), BF16),
        dma((2,)), dma((2,)),
        dma((8,)), dma((8,)),
        dma((16,)), dma((16,)),
        dma((16,)), dma((16,)),
        dma((16,)), dma((16,)),
        dma((16,)), dma((16,)),
        dma((1,)), dma((1,)),
    ]
    return pl.pallas_call(
        kernel,
        out_shape=jax.ShapeDtypeStruct((1, 1, ATOMS, CH), F32),
        in_specs=[vmem] * 6 + [smem] + [vmem] * 5,
        out_specs=vmem,
        scratch_shapes=scratch,
        compiler_params=pltpu.CompilerParams(
            collective_id=0, has_side_effects=True, vmem_limit_bytes=40 * 1024 * 1024
        ),
    )(features, offsets, species, neighbours, edge_mask, wavevectors, wavevectors, vw, radw, emb, mixw, gf)


def solution(mesh):
    block = P("gx", "gy", None, None)
    placed = (block, block, P("gx", "gy", None), block, block, P(), P(), P(), P(), P(), P("gx", None, None))
    return jax.shard_map(shards, mesh=mesh, in_specs=placed, out_specs=block, check_vma=False)
```

time: 189 us -> 65.5 us (0.35)
  waiting for transfers between devices: 81.8 us -> 0 us
  Pallas kernels: 0 us -> 57.5 us
  starting transfers between devices: 52.5 us -> 0 us
  local copies, waits for them, and re-layouts: 28.3 us -> 7.5 us
  matrix products: 18 us -> 0 us
  other arithmetic: 6.77 us -> 0 us
    pallas_call x0 -> x1, Pallas kernels: none -> 57.5 us  [shards(): pl.pallas_call(kernel, out_shape=jax.ShapeDtypeStruct((1, 1, ATOMS, CH),...]
    ppermute x8 -> x0, waiting for transfers between devices: 49.2 us -> none  [the longest x4 41 us: padded(): lax.ppermute(head, axis, [((i + 1) % count, i) for i in range(count)])]
    all_to_all x3 -> x0, starting transfers between devices: 34.9 us -> none  [the longest x2 18 us: from_everyone(): lax.all_to_all(jnp.broadcast_to(shard[None], (count, *shard.shape)), axis...]
    all_to_all x3 -> x0, waiting for transfers between devices: 32.6 us -> none  [the longest x2 32.6 us: from_everyone(): lax.all_to_all(jnp.broadcast_to(shard[None], (count, *shard.shape)), axis...]
    dot_general x11 -> x0, matrix products: 18 us -> none  [the longest x2 5.09 us: contract_atoms(): lax.dot_general(table, feats, (((0,), (0,)), ((), ())), precision=HIGHEST...]
    ppermute x8 -> x0, starting transfers between devices: 17.6 us -> none  [the longest x4 11.4 us: padded(): lax.ppermute(head, axis, [((i + 1) % count, i) for i in range(count)])]
    gather x6 -> x0, local copies, waits for them, and re-layouts: 11 us -> none  [the longest x2 4.49 us: edge_block(): flat_values[row_index]]
    while x38 -> x0, local copies, waits for them, and re-layouts: 8.19 us -> none
  transfers between devices with their start and end apart: 11 -> 0, of which waited for: 5 -> 0; matrix products, arithmetic and copies ran while one was open for 17% -> 0% of each run, Pallas kernels for 0% -> 0%
where the time goes in v1:
time: 65.5 us; the launch traced here: 65.1 us
  Pallas kernels  57.5 us (88%)
  local copies, waits for them, and re-layouts  7.5 us (11%)
    pallas_call x1, Pallas kernels, shards(): pl.pallas_call(kernel, out_shape=jax.ShapeDtypeStruct((1, 1, ATOMS, CH),...  57.5 us
    unnamed x20, local copies, waits for them, and re-layouts  7.5 us

profile of v1, /device:TPU:1, one launch (start us, length us, event | category | flops | bytes accessed | tf_op | source)
XLA Modules:
  0.0 65.1 jit_solution(8430241840542144767)
XLA Ops:
  0.0 0.0 copy-start.3
  0.0 0.7 %copy.12.offs = f32[1,1,3,128]{3,2,1,0:T(4,128)S(1)} copy(f32[1,1,3,128]{3,1,2,0:T(1,128)} %param.12) | data formatting | bytes 3072 | tf_op args[1]
  0.7 0.8 %copy.13.neigh = s32[1,1,128,8]{3,2,1,0:T(8,128)S(1)} copy(s32[1,1,128,8]{2,3,1,0:T(8,128)} %param.14) | data formatting | bytes 8192 | tf_op args[3]
  1.5 0.0 copy-start.6
  1.5 0.0 copy-start.7
  1.5 0.8 %copy.14.mask = s32[1,1,128,8]{3,2,1,0:T(8,128)S(1)} copy(s32[1,1,128,8]{2,3,1,0:T(8,128)} %param.15) | data formatting | bytes 8192 | tf_op args[4]
  2.3 0.0 copy-done.3
  2.3 0.0 copy-done.6
  2.3 0.0 copy-done.7
  2.3 0.0 copy-start
  2.4 0.9 %copy-done = f32[256,256]{1,0:T(8,128)S(1)} copy-done((f32[256,256]{1,0:T(8,128)S(1)}, f32[256,256]{1,0:T(8,128)}, u32[]{:S(2)}) %copy-start) | copy-done | bytes 262168
  3.3 0.0 copy-start.1
  3.3 0.9 %copy-done.1 = f32[256,256]{1,0:T(8,128)S(1)} copy-done((f32[256,256]{1,0:T(8,128)S(1)}, f32[256,256]{1,0:T(8,128)}, u32[]{:S(2)}) %copy-start.1) | copy-done | bytes 262168
  4.3 0.0 copy-start.2
  4.3 0.9 %copy-done.2 = f32[1,256,256]{2,1,0:T(8,128)S(1)} copy-done((f32[1,256,256]{2,1,0:T(8,128)S(1)}, f32[1,256,256]{2,1,0:T(8,128)}, u32[]{:S(2)}) %copy-start.2) | copy-done | bytes 262168
  5.2 0.0 copy-start.4
  5.2 0.8 %copy-done.4 = f32[64,256]{1,0:T(8,128)S(1)} copy-done((f32[64,256]{1,0:T(8,128)S(1)}, f32[64,256]{1,0:T(8,128)}, u32[]{:S(2)}) %copy-start.4) | copy-done | bytes 65560
  6.0 0.0 copy-start.5
  6.0 0.8 %copy-done.5 = f32[64,256]{1,0:T(8,128)S(1)} copy-done((f32[64,256]{1,0:T(8,128)S(1)}, f32[64,256]{1,0:T(8,128)}, u32[]{:S(2)}) %copy-start.5) | copy-done | bytes 65560
  6.9 57.5 %shard_map.109 = f32[1,1,128,256]{3,2,1,0:T(8,128)S(1)} custom-call(f32[1,1,128,256]{3,2,1,0:T(8,128)S(1)} %copy-done.3, f32[1,1,3,128]{3,2,1,0:T(4,128)S(1)} %copy.12.offs, s32[1,1,128]{2,1,0:T(1,128)S(1)} %copy-done.7, s32[1,1,128,8]{3,2,1,0:T(8,128)S(1)} %copy.13.neigh, s32[1,1,128,8]{3,2,1,0:T(8,128)S(1)} %copy.14.mask, s32[3,512]{1,0:T(4,128)S(1)} %copy-done.6, ...), custom_call_target="tpu_custom_call" | custom-call | tf_op jit(solution)/shard_map/pallas_call | solution.py:360
  64.4 0.7 %copy.16 = f32[1,1,128,256]{3,2,1,0:T(8,128)} copy(f32[1,1,128,256]{3,2,1,0:T(8,128)S(1)} %shard_map.109) | data formatting | bytes 262144
Async XLA Ops:
  0.0 2.3 %copy-start.3 = (f32[1,1,128,256]{3,2,1,0:T(8,128)S(1)}, f32[1,1,128,256]{3,2,1,0:T(8,128)}, u32[]{:S(2)}) copy-start(f32[1,1,128,256]{3,2,1,0:T(8,128)} %feat.1) | copy-start | bytes 393220
  1.5 0.8 %copy-start.6 = (s32[3,512]{1,0:T(4,128)S(1)}, s32[3,512]{1,0:T(4,128)}, u32[]{:S(2)}) copy-start(s32[3,512]{1,0:T(4,128)} %wv_s.1) | copy-start | bytes 18436
  1.5 0.8 %copy-start.7 = (s32[1,1,128]{2,1,0:T(1,128)S(1)}, s32[1,1,128]{2,1,0:T(1,128)}, u32[]{:S(2)}) copy-start(s32[1,1,128]{2,1,0:T(1,128)} %spec.1) | copy-start | bytes 1540
  2.3 1.0 %copy-start = (f32[256,256]{1,0:T(8,128)S(1)}, f32[256,256]{1,0:T(8,128)}, u32[]{:S(2)}) copy-start(f32[256,256]{1,0:T(8,128)} %vw.1) | copy-start | bytes 786436
  3.3 0.9 %copy-start.1 = (f32[256,256]{1,0:T(8,128)S(1)}, f32[256,256]{1,0:T(8,128)}, u32[]{:S(2)}) copy-start(f32[256,256]{1,0:T(8,128)} %mixw.1) | copy-start | bytes 786436
  4.3 0.9 %copy-start.2 = (f32[1,256,256]{2,1,0:T(8,128)S(1)}, f32[1,256,256]{2,1,0:T(8,128)}, u32[]{:S(2)}) copy-start(f32[1,256,256]{2,1,0:T(8,128)} %gf.1) | copy-start | bytes 786436
  5.2 0.8 %copy-start.4 = (f32[64,256]{1,0:T(8,128)S(1)}, f32[64,256]{1,0:T(8,128)}, u32[]{:S(2)}) copy-start(f32[64,256]{1,0:T(8,128)} %radw.1) | copy-start | bytes 196612
  6.0 0.8 %copy-start.5 = (f32[64,256]{1,0:T(8,128)S(1)}, f32[64,256]{1,0:T(8,128)}, u32[]{:S(2)}) copy-start(f32[64,256]{1,0:T(8,128)} %emb.1) | copy-start | bytes 196612

commit v2 on v1

v2 whole, which is shorter than its diff:
```python
import math

import jax
import jax.numpy as jnp
from jax import lax
from jax.experimental import pallas as pl
from jax.experimental.pallas import tpu as pltpu
from jax.sharding import PartitionSpec as P

MESH = pl.DeviceIdType.MESH
F32 = jnp.float32
BF16 = jnp.bfloat16

GX = 32
GY = 16
NZ = 16
ATOMS = 128
CH = 256
MODES = 512
SLOTS = 8
RADIAL = 64
SCALE = 1.0 / math.sqrt(33554432)
TURN = 2.0 * math.pi

PLANE_ORDER = (10, 9, 11, 6, 14, 8, 2, 5, 7, 13, 15, 4, 12, 1, 3)

COS_TERMS = [(-1.0) ** n * TURN ** (2 * n) / math.factorial(2 * n) for n in range(7)]
SIN_TERMS = [(-1.0) ** n * TURN ** (2 * n + 1) / math.factorial(2 * n + 1) for n in range(7)]


def halves(x):
    hi = x.astype(BF16)
    return hi, (x - hi.astype(F32)).astype(BF16)


def mm(a, b):
    return jnp.dot(a, b, preferred_element_type=F32)


def mm3(a_hi, a_lo, b_hi, b_lo):
    return mm(a_hi, b_hi) + (mm(a_hi, b_lo) + mm(a_lo, b_hi))


def cos_sin(turns):
    q = jnp.floor(turns * 2.0 + 0.5)
    r = turns - q * 0.5
    h = q * 0.5
    sign = 1.0 - 4.0 * (h - jnp.floor(h))
    y = r * r
    c = jnp.full_like(y, COS_TERMS[6])
    s = jnp.full_like(y, SIN_TERMS[6])
    for n in range(5, -1, -1):
        c = c * y + COS_TERMS[n]
        s = s * y + SIN_TERMS[n]
    return c * sign, s * (r * sign)


def remote(src, dst, send, recv, gx, gy):
    return pltpu.make_async_remote_copy(
        src_ref=src, dst_ref=dst, send_sem=send, recv_sem=recv, device_id=(gx, gy), device_id_type=MESH
    )


def kernel(
    feat_h, offs_h, spec_h, neigh_h, mask_h, wv_h, vw_h, radw_h, emb_h, mixw_h, gf_h,
    out,
    feat, offs, spec, neigh, mask, wv, vw, embed, mixw, gf,
    carry2, halo, tf, tt_hi, tt_lo, ncol, wpad,
    part, theirs, got0, got1, sums, got2, rows16, filt1, filt2, filt3, rh_hi, rh_lo, lsum, lpeer, lgot,
    dist, spj, rowid, onehot, bh, bl, filt, wcat, mix_hi, mix_lo, vb,
    ready, s_in, s_pair, r_pair, s_halo, r_halo, s_rs1, r_rs1, s_rs2, r_rs2, s_ag1, r_ag1, s_ag2, r_ag2,
):
    gx = lax.axis_index("gx")
    gy = lax.axis_index("gy")
    c = lax.rem(gx, 2)
    z = gx // 2
    px = gy // 4
    py = lax.rem(gy, 4)
    peer = gx + 1 - 2 * c
    other = lax.rem(gx + 31 + 2 * c, GX)
    up = lax.rem(gy + 1, GY)
    down = lax.rem(gy + GY - 1, GY)

    def plane(k):
        return lax.rem(px + k // 4, 4) * 4 + lax.rem(py + k % 4, 4)

    def column(k):
        return 2 * lax.rem(z + k, NZ) + c

    barrier = pltpu.get_barrier_semaphore()
    greeted = [(column(k), gy) for k in (4, 12, 3, 13, 2, 14, 1, 15)]
    greeted += [(gx, plane(k)) for k in PLANE_ORDER]
    greeted += [(other, gy), (peer, gy)]
    for device in greeted:
        pl.semaphore_signal(barrier, inc=1, device_id=device, device_id_type=MESH)

    loads = [
        pltpu.make_async_copy(src, dst, s_in.at[i])
        for i, (src, dst) in enumerate((
            (wv_h, wv), (offs_h.at[0], offs), (feat_h.at[0, 0], feat), (spec_h, spec), (vw_h, vw),
            (neigh_h.at[0, 0], neigh), (mask_h.at[0, 0], mask), (radw_h, embed.at[pl.ds(0, RADIAL)]),
            (emb_h, embed.at[pl.ds(RADIAL, RADIAL)]), (mixw_h, mixw), (gf_h.at[0], gf),
        ))
    ]
    for load in loads:
        load.start()
    for load in loads[0:3]:
        load.wait()

    wpad[...] = jnp.zeros(wpad.shape, F32)
    vectors = wv[...].astype(F32)
    wpad[0:3, :] = vectors
    r = lax.broadcasted_iota(jnp.int32, (MODES, MODES), 0)
    m = lax.broadcasted_iota(jnp.int32, (MODES, MODES), 1)
    group = 2 * ((z + 4 + 8 * ((r >> 7) & 1) + (r & 7)) & 15) + (c ^ (r >> 8))
    pick = jnp.where(group * 16 + ((r >> 3) & 15) == m, 1.0, 0.0).astype(BF16)
    ncol[...] = lax.dot_general(
        pick, wpad[...].astype(BF16), (((1,), (1,)), ((), ())), preferred_element_type=F32
    )

    def table(i, block, positions):
        n = ncol[pl.ds(pl.multiple_of(i * 64, 64), 64), :]
        n0, n1, n2 = n[:, 0:1], n[:, 1:2], n[:, 2:3]
        w0 = (n0.astype(jnp.int32) * block & 31).astype(F32)
        w1 = (n1.astype(jnp.int32) * gy & 15).astype(F32)
        turns = (w0 + n0 * positions[0]) * (1.0 / 32)
        turns = turns + (w1 + n1 * positions[1]) * (1.0 / 16)
        turns = turns + n2 * positions[2]
        return jnp.concatenate(cos_sin(turns), axis=0)

    f_hi, f_lo = halves(feat[...])

    def own_table(i):
        both = table(i, gx, [offs[0], offs[1], offs[2]])
        t_hi, t_lo = halves(both)
        return both, mm3(t_hi, t_lo, f_hi, f_lo)

    def mine_step(i, carry):
        both, p = own_table(i)
        tf[i, :, 0:ATOMS] = both
        part[i, :, :, 0:CH] = p[0:64].reshape(8, 8, CH)
        part[i, :, :, CH:2 * CH] = p[64:128].reshape(8, 8, CH)
        return carry

    def theirs_step(i, carry):
        _, p = own_table(i + 4)
        theirs[i, :, :, 0:CH] = p[0:64].reshape(8, 8, CH)
        theirs[i, :, :, CH:2 * CH] = p[64:128].reshape(8, 8, CH)
        return carry

    lax.fori_loop(0, 4, theirs_step, 0)
    lax.fori_loop(0, 4, mine_step, 0)

    sends = []

    def start(src, dst, s_sems, r_sems, i, x, y):
        copy = remote(src, dst, s_sems.at[i], r_sems.at[i], x, y)
        copy.start()
        sends.append(copy)

    def arrived(dst, r_sems, i):
        remote(dst, dst, s_pair.at[0], r_sems.at[i], peer, gy).wait_recv()

    def drain():
        while sends:
            sends.pop().wait_send()

    pl.semaphore_wait(barrier, len(greeted))
    for k in (4, 12):
        pl.semaphore_signal(ready, inc=1, device_id=(column(k), gy), device_id_type=MESH)
    for q in range(2):
        start(theirs.at[pl.ds(2 * q, 2)], got0.at[pl.ds(2 * q, 2)], s_pair, r_pair, q, peer, gy)

    for q in range(2):
        arrived(got0.at[pl.ds(2 * q, 2)], r_pair, q)
        part[2 * q:2 * q + 2] = part[2 * q:2 * q + 2] + got0[2 * q:2 * q + 2]
        for k in PLANE_ORDER:
            to = plane(k)
            start(part.at[2 * q + to // 8, lax.rem(to, 8)], got1.at[q, k], s_rs1, r_rs1, 16 * q + k, gx, to)

    for load in loads[3:5]:
        load.wait()
    vw_hi, vw_lo = halves(vw[...])
    halo[4, 0:CH, :] = jnp.transpose(mm3(f_hi, f_lo, vw_hi, vw_lo))
    halo[4, CH:CH + 8, :] = jnp.zeros((8, ATOMS), F32)
    for i in range(3):
        halo[4, CH + i:CH + i + 1, :] = offs[i]
    halo[4, CH + 3:CH + 4, :] = spec[0].astype(F32)
    start(halo.at[4, pl.ds(CH, 8)], carry2, s_pair, r_pair, 2, peer, gy)
    start(halo.at[4], halo.at[7 - 6 * c], s_halo, r_halo, 1, other, gy)
    start(halo.at[4], halo.at[1 + 6 * c], s_halo, r_halo, 0, peer, gy)
    pl.semaphore_wait(ready, 2)

    for q in range(2):
        total = part[2 * q + gy // 8, lax.rem(gy, 8)]
        for k in range(1, 16):
            arrived(got1.at[q, k], r_rs1, 16 * q + k)
            total = total + got1[q, k]
        for k in range(8):
            sums[8 * q + k] = total[k:k + 1, :]
        for k in (4, 3, 5, 2, 6, 1, 7, 0):
            d = (4 + 8 * q + k) % 16
            if d:
                start(sums.at[8 * q + k], got2.at[d], s_rs2, r_rs2, d, column(d), gy)

    arrived(halo.at[7 - 6 * c], r_halo, 0)
    arrived(halo.at[1 + 6 * c], r_halo, 1)
    for i in range(3):
        start(halo.at[3 * i + 1], halo.at[3 * i], s_halo, r_halo, 2 + i, gx, up)
        start(halo.at[3 * i + 1], halo.at[3 * i + 2], s_halo, r_halo, 5 + i, gx, down)

    for load in loads[5:]:
        load.wait()
    mine = lax.broadcasted_iota(jnp.int32, (3, MODES), 1) == gx * 16 + gy
    wave = jnp.sum(jnp.where(mine, vectors, 0.0), axis=1, keepdims=True)
    wave0 = wave[0:1] * (TURN / 32)
    wave1 = wave[1:2] * (TURN / 16)
    wave2 = wave[2:3] * TURN
    damp = jnp.exp(-0.01 * (wave0 * wave0 + wave1 * wave1 + wave2 * wave2)) * SCALE
    gf_hi, gf_lo = halves(gf[...])
    rows16[...] = jnp.zeros(rows16.shape, F32)

    arrived(carry2, r_pair, 2)

    def peer_step(i, carry):
        tf[i, :, ATOMS:2 * ATOMS] = table(i, peer, [carry2[0:1], carry2[1:2], carry2[2:3]])
        return carry

    lax.fori_loop(0, 4, peer_step, 0)
    for i in range(4):
        hi, lo = halves(jnp.transpose(tf[i]))
        tt_hi[i // 2, :, 128 * (i % 2):128 * (i % 2) + 128] = hi
        tt_lo[i // 2, :, 128 * (i % 2):128 * (i % 2) + 128] = lo
    wt = jnp.transpose(embed[...])
    hi, lo = halves(wt)
    wcat[:, 0:128] = hi
    wcat[:, 128:256] = lo
    hi, lo = halves(jnp.transpose(mixw[...]))
    mix_hi[...] = hi
    mix_lo[...] = lo

    listed = jnp.where(mask[...] > 0, neigh[...], -1)
    source = listed >> 7
    atom = listed & 127
    s = (((source >> 4) - gx + 1) & 31) - 1
    t = (((source & 15) - gy + 1) & 15) - 1
    near = (s + 1) * 3 + (t + 1)
    rowid[...] = jnp.where(listed < 0, -1, near * ATOMS + atom)

    def onehot_step(e, carry):
        lanes = pl.ds(pl.multiple_of(e * ATOMS, ATOMS), ATOMS)
        place = rowid[pl.ds(e, 1), :]
        at = lax.broadcasted_iota(jnp.int32, (ATOMS, ATOMS), 0)
        for j in range(9):
            hit = jnp.where(at == place - ATOMS * j, 1.0, 0.0)
            onehot[ATOMS * j:ATOMS * j + ATOMS, lanes] = hit.astype(BF16)
        return carry

    lax.fori_loop(0, SLOTS, onehot_step, 0)

    total = sums[12]
    for k in (1, 15, 2, 14, 3, 13, 4, 12, 5, 11, 6, 10, 7, 9, 8):
        arrived(got2.at[k], r_rs2, k)
        total = total + got2[k]
    rows16[0:1, :] = total[:, 0:CH]
    rows16[1:2, :] = total[:, CH:2 * CH]
    a_hi, a_lo = halves(rows16[...])
    mixed = mm3(a_hi, a_lo, gf_hi, gf_lo)
    filt1[12, :, 0:CH] = mixed[0:1, :] * damp
    filt1[12, :, CH:2 * CH] = mixed[1:2, :] * damp
    for d in (8, 7, 9, 6, 10, 5, 11, 4, 12, 3, 13, 2, 14, 1, 15):
        at = (12 - d) % 16
        start(filt1.at[12], filt1.at[at], s_ag1, r_ag1, at, column(d), gy)

    for i in range(3):
        arrived(halo.at[3 * i], r_halo, 2 + i)
        arrived(halo.at[3 * i + 2], r_halo, 5 + i)
    found = [jnp.zeros((SLOTS, ATOMS), F32) for _ in range(4)]
    for j in range(9):
        for i in range(4):
            row = jnp.broadcast_to(halo[j, CH + i:CH + i + 1, :], (SLOTS, ATOMS))
            taken = jnp.take_along_axis(row, atom, axis=1)
            found[i] = jnp.where(near == j, taken, found[i])
    own = halo[4, CH:CH + 8, :]
    gap0 = (s.astype(F32) + found[0]) - own[0:1, :]
    gap1 = (t.astype(F32) + found[1]) - own[1:2, :]
    gap2 = found[2] - own[2:3, :]
    dist[...] = jnp.sqrt(gap0 * gap0 + gap1 * gap1 + gap2 * gap2 + 0.01)
    spj[...] = found[3]
    own_kind = own[3:4, :]

    def basis_step(e, carry):
        lanes = pl.ds(pl.multiple_of(e * ATOMS, ATOMS), ATOMS)
        k = lax.broadcasted_iota(jnp.int32, (RADIAL, ATOMS), 0).astype(F32)
        scaled = (dist[pl.ds(e, 1), :] - k * (3.0 / 63)) / (6.0 / 63)
        hi, lo = halves(jnp.exp(-scaled * scaled))
        kinds = jnp.where(k == spj[pl.ds(e, 1), :], 1.0, 0.0) + jnp.where(k == own_kind, 1.0, 0.0)
        kinds = kinds.astype(BF16)
        bh[0:64, lanes] = hi
        bh[64:128, lanes] = kinds
        bh[128:192, lanes] = hi
        bh[192:256, lanes] = kinds
        bl[:, lanes] = lo
        return carry

    lax.fori_loop(0, SLOTS, basis_step, 0)

    def filter_step(e, carry):
        lanes = pl.ds(pl.multiple_of(e * 256, 256), 256)
        before = mm(wcat[...], bh[:, lanes]) + mm(wcat[:, 0:64], bl[:, lanes])
        hi, lo = halves(before / (1.0 + jnp.exp(-before)))
        filt[:, lanes] = mm3(mix_hi[...], mix_lo[...], hi, lo)
        return carry

    lax.fori_loop(0, 4, filter_step, 0)
    drain()

    def spread(q):
        for k in range(8):
            at = 8 * q + k
            if at != 12:
                arrived(filt1.at[at], r_ag1, at)
            filt2[q, k:k + 1, :] = filt1[at]
        for k in PLANE_ORDER:
            start(filt2.at[q], filt3.at[q, gy], s_ag2, r_ag2, 16 * q + k, gx, plane(k))
        filt3[q, gy] = filt2[q]

    spread(1)
    spread(0)

    for j in range(9):
        hi, lo = halves(halo[j, 0:CH, :])
        vb[0:CH, ATOMS * j:ATOMS * j + ATOMS] = hi
        vb[CH:2 * CH, ATOMS * j:ATOMS * j + ATOMS] = lo

    def gather_step(e, acc):
        lanes = pl.ds(pl.multiple_of(e * 256, 256), 256)
        g = mm(vb[...], onehot[:, lanes])
        msg = (g[0:CH] + g[CH:2 * CH]) * filt[:, lanes]
        return acc + (msg[:, 0:ATOMS] + msg[:, ATOMS:2 * ATOMS])

    short = lax.fori_loop(0, 4, gather_step, jnp.zeros((CH, ATOMS), F32))
    out[0, 0] = jnp.transpose(short) * (1.0 / math.sqrt(SLOTS))

    def factors(q):
        for k in range(1, 16):
            sender = lax.rem(px + 4 - k // 4, 4) * 4 + lax.rem(py + 4 - k % 4, 4)
            arrived(filt3.at[q, sender], r_ag2, 16 * q + k)
        for h in range(2):
            hi, lo = halves(filt3[q, 8 * h:8 * h + 8].reshape(64, 2 * CH))
            for at, lane in ((128 * h, 0), (128 * h + 64, CH)):
                rh_hi[at:at + 64, :] = hi[:, lane:lane + CH]
                rh_lo[at:at + 64, :] = lo[:, lane:lane + CH]

    def terms(q, rows):
        return mm3(tt_hi[q, rows], tt_lo[q, rows], rh_hi[...], rh_lo[...])

    near_rows, far_rows = slice(0, ATOMS), slice(ATOMS, 2 * ATOMS)
    factors(1)
    lsum[...] = terms(1, far_rows)
    out[0, 0] += terms(1, near_rows)
    drain()
    factors(0)
    lpeer[...] = lsum[...] + terms(0, far_rows)
    start(lpeer, lgot, s_pair, r_pair, 3, peer, gy)
    base = out[0, 0] + terms(0, near_rows)
    arrived(lgot, r_pair, 3)
    out[0, 0] = base + lgot[...]
    drain()


def shards(features, offsets, species, neighbours, edge_mask, wavevectors, vw, radw, emb, mixw, gf):
    vmem = pl.BlockSpec(memory_space=pltpu.VMEM)
    hbm = pl.BlockSpec(memory_space=pltpu.HBM)
    dma = pltpu.SemaphoreType.DMA
    scratch = [
        pltpu.VMEM((ATOMS, CH), F32),
        pltpu.VMEM((3, 1, ATOMS), F32),
        pltpu.VMEM((1, 1, ATOMS), jnp.int32),
        pltpu.VMEM((SLOTS, ATOMS), jnp.int32),
        pltpu.VMEM((SLOTS, ATOMS), jnp.int32),
        pltpu.VMEM((3, MODES), jnp.int32),
        pltpu.VMEM((CH, CH), F32),
        pltpu.VMEM((2 * RADIAL, CH), F32),
        pltpu.VMEM((CH, CH), F32),
        pltpu.VMEM((CH, CH), F32),
        pltpu.VMEM((8, ATOMS), F32),
        pltpu.VMEM((9, CH + 8, ATOMS), F32),
        pltpu.VMEM((4, 128, 2 * ATOMS), F32),
        pltpu.VMEM((2, 2 * ATOMS, 256), BF16),
        pltpu.VMEM((2, 2 * ATOMS, 256), BF16),
        pltpu.VMEM((MODES, 128), F32),
        pltpu.VMEM((128, MODES), F32),
        pltpu.VMEM((4, 8, 8, 2 * CH), F32),
        pltpu.VMEM((4, 8, 8, 2 * CH), F32),
        pltpu.VMEM((4, 8, 8, 2 * CH), F32),
        pltpu.VMEM((2, GY, 8, 2 * CH), F32),
        pltpu.VMEM((NZ, 1, 2 * CH), F32),
        pltpu.VMEM((NZ, 1, 2 * CH), F32),
        pltpu.VMEM((16, CH), F32),
        pltpu.VMEM((NZ, 1, 2 * CH), F32),
        pltpu.VMEM((2, 8, 2 * CH), F32),
        pltpu.VMEM((2, GY, 8, 2 * CH), F32),
        pltpu.VMEM((256, CH), BF16),
        pltpu.VMEM((256, CH), BF16),
        pltpu.VMEM((ATOMS, CH), F32),
        pltpu.VMEM((ATOMS, CH), F32),
        pltpu.VMEM((ATOMS, CH), F32),
        pltpu.VMEM((SLOTS, ATOMS), F32),
        pltpu.VMEM((SLOTS, ATOMS), F32),
        pltpu.VMEM((SLOTS, ATOMS), jnp.int32),
        pltpu.VMEM((9 * ATOMS, SLOTS * ATOMS), BF16),
        pltpu.VMEM((256, SLOTS * ATOMS), BF16),
        pltpu.VMEM((64, SLOTS * ATOMS), BF16),
        pltpu.VMEM((CH, SLOTS * ATOMS), F32),
        pltpu.VMEM((CH, 256), BF16),
        pltpu.VMEM((CH, CH), BF16),
        pltpu.VMEM((CH, CH), BF16),
        pltpu.VMEM((2 * CH, 9 * ATOMS), BF16),
        pltpu.SemaphoreType.REGULAR,
        dma((11,)),
        dma((4,)), dma((4,)),
        dma((8,)), dma((8,)),
        dma((32,)), dma((32,)),
        dma((16,)), dma((16,)),
        dma((16,)), dma((16,)),
        dma((32,)), dma((32,)),
    ]
    return pl.pallas_call(
        kernel,
        out_shape=jax.ShapeDtypeStruct((1, 1, ATOMS, CH), F32),
        in_specs=[hbm] * 11,
        out_specs=vmem,
        scratch_shapes=scratch,
        compiler_params=pltpu.CompilerParams(
            collective_id=0, has_side_effects=True, vmem_limit_bytes=56 * 1024 * 1024
        ),
    )(
        features, jnp.transpose(offsets, (0, 2, 1, 3)), species, jnp.swapaxes(neighbours, 2, 3),
        jnp.swapaxes(edge_mask, 2, 3), wavevectors, vw, radw, emb, mixw, gf,
    )


def solution(mesh):
    block = P("gx", "gy", None, None)
    placed = (block, block, P("gx", "gy", None), block, block, P(), P(), P(), P(), P(), P("gx", None, None))
    return jax.shard_map(shards, mesh=mesh, in_specs=placed, out_specs=block, check_vma=False)
```

time: 65.5 us -> 54.2 us (0.83)
  local copies, waits for them, and re-layouts: 7.5 us -> 1.57 us
  Pallas kernels: 57.5 us -> 52.5 us
    unnamed x20 -> x1, local copies, waits for them, and re-layouts: 7.5 us -> 1.57 us
    pallas_call x1, Pallas kernels: 57.5 us -> 52.5 us  [shards(): pl.pallas_call(kernel, out_shape=jax.ShapeDtypeStruct((1, 1, ATOMS, CH),...]
where the time goes in v2:
time: 54.2 us; the launch traced here: 54.1 us
  Pallas kernels  52.5 us (97%)
  local copies, waits for them, and re-layouts  1.57 us (3%)
    pallas_call x1, Pallas kernels, shards(): pl.pallas_call(kernel, out_shape=jax.ShapeDtypeStruct((1, 1, ATOMS, CH),...  52.5 us
    unnamed x1, local copies, waits for them, and re-layouts  1.57 us

profile of v2, /device:TPU:1, one launch (start us, length us, event | category | flops | bytes accessed | tf_op | source)
XLA Modules:
  0.0 54.1 jit_solution(8734370491212032719)
XLA Ops:
  0.0 52.5 %shard_map.109 = f32[1,1,128,256]{3,2,1,0:T(8,128)} custom-call(f32[1,1,128,256]{3,2,1,0:T(8,128)} %feat_h.1, f32[1,3,1,128]{3,2,1,0:T(1,128)} %bitcast.5, s32[1,1,128]{2,1,0:T(1,128)} %spec_h.1, s32[1,1,8,128]{3,2,1,0:T(8,128)} %bitcast.3, s32[1,1,8,128]{3,2,1,0:T(8,128)} %bitcast.4, s32[3,512]{1,0:T(4,128)} %wv_h.1, f32[256,256]{1,0:T(8,128)} %vw_h.1, ...), custom_call_target="tpu_custom_call" | custom-call | tf_op jit(solution)/shard_map/pallas_call | solution.py:429
  52.5 1.6 %copy.13 = f32[1,1,128,256]{3,2,1,0:T(8,128)} copy(f32[1,1,128,256]{3,2,1,0:T(8,128)} %shard_map.109) | data formatting | bytes 262144

commit v3 on v2

--- a/solution.py
+++ b/solution.py
@@ -65,10 +65,10 @@
     feat_h, offs_h, spec_h, neigh_h, mask_h, wv_h, vw_h, radw_h, emb_h, mixw_h, gf_h,
     out,
     feat, offs, spec, neigh, mask, wv, vw, embed, mixw, gf,
-    carry2, halo, tf, tt_hi, tt_lo, ncol, wpad,
+    near_pos, halo, tf, tt_hi, tt_lo, ncol, wpad,
     part, theirs, got0, got1, sums, got2, rows16, filt1, filt2, filt3, rh_hi, rh_lo, lsum, lpeer, lgot,
     dist, spj, rowid, onehot, bh, bl, filt, wcat, mix_hi, mix_lo, vb,
-    ready, s_in, s_pair, r_pair, s_halo, r_halo, s_rs1, r_rs1, s_rs2, r_rs2, s_ag1, r_ag1, s_ag2, r_ag2,
+    ready, s_in, s_pair, r_pair, s_pos, r_pos, s_halo, r_halo, s_rs1, r_rs1, s_rs2, r_rs2, s_ag1, r_ag1, s_ag2, r_ag2,
 ):
     gx = lax.axis_index("gx")
     gy = lax.axis_index("gy")
@@ -87,10 +87,21 @@
     def column(k):
         return 2 * lax.rem(z + k, NZ) + c
 
+    to_peer, to_other = 3 * (2 * c), 3 * (2 - 2 * c)
+    around = [
+        (peer, gy, to_peer + 1), (peer, up, to_peer), (peer, down, to_peer + 2),
+        (other, gy, to_other + 1), (other, up, to_other), (other, down, to_other + 2),
+        (gx, up, 3), (gx, down, 5),
+    ]
+    from_peer, from_other = to_other, to_peer
+    slots_here = [
+        from_peer + 1, from_peer, from_peer + 2, from_other + 1, from_other, from_other + 2, 3, 5,
+    ]
+
     barrier = pltpu.get_barrier_semaphore()
     greeted = [(column(k), gy) for k in (4, 12, 3, 13, 2, 14, 1, 15)]
     greeted += [(gx, plane(k)) for k in PLANE_ORDER]
-    greeted += [(other, gy), (peer, gy)]
+    greeted += [(other, up), (other, down), (peer, up), (peer, down), (other, gy), (peer, gy)]
     for device in greeted:
         pl.semaphore_signal(barrier, inc=1, device_id=device, device_id_type=MESH)
 
@@ -104,23 +115,31 @@
     ]
     for load in loads:
         load.start()
-    for load in loads[0:3]:
+    for load in loads[0:4]:
         load.wait()
+    near_pos[4] = jnp.zeros((8, ATOMS), F32)
+    for i in range(3):
+        near_pos[4, i:i + 1, :] = offs[i]
+    near_pos[4, 3:4, :] = spec[0].astype(F32)
 
     wpad[...] = jnp.zeros(wpad.shape, F32)
     vectors = wv[...].astype(F32)
     wpad[0:3, :] = vectors
-    r = lax.broadcasted_iota(jnp.int32, (MODES, MODES), 0)
-    m = lax.broadcasted_iota(jnp.int32, (MODES, MODES), 1)
-    group = 2 * ((z + 4 + 8 * ((r >> 7) & 1) + (r & 7)) & 15) + (c ^ (r >> 8))
-    pick = jnp.where(group * 16 + ((r >> 3) & 15) == m, 1.0, 0.0).astype(BF16)
+    even = wpad[0:8, :]
+    odd = pltpu.roll(even, MODES - 16, 1)
+    wpad[0:8, :] = jnp.where(c == 0, even, odd)
+    wpad[8:16, :] = jnp.where(c == 0, odd, even)
+    r = lax.broadcasted_iota(jnp.int32, (256, 1), 0)
+    m = lax.broadcasted_iota(jnp.int32, (256, MODES), 1)
+    target = 32 * ((z + 4 + 8 * (r >> 7) + (r & 7)) & 15) + ((r >> 3) & 15)
+    pick = jnp.where(m == target, 1.0, 0.0).astype(BF16)
     ncol[...] = lax.dot_general(
         pick, wpad[...].astype(BF16), (((1,), (1,)), ((), ())), preferred_element_type=F32
     )
 
-    def table(i, block, positions):
+    def table(i, parity, block, positions):
         n = ncol[pl.ds(pl.multiple_of(i * 64, 64), 64), :]
-        n0, n1, n2 = n[:, 0:1], n[:, 1:2], n[:, 2:3]
+        n0, n1, n2 = [n[:, 8 * parity + a:8 * parity + a + 1] for a in range(3)]
         w0 = (n0.astype(jnp.int32) * block & 31).astype(F32)
         w1 = (n1.astype(jnp.int32) * gy & 15).astype(F32)
         turns = (w0 + n0 * positions[0]) * (1.0 / 32)
@@ -130,26 +149,20 @@
 
     f_hi, f_lo = halves(feat[...])
 
-    def own_table(i):
-        both = table(i, gx, [offs[0], offs[1], offs[2]])
+    def own_table(i, parity, into):
+        both = table(i, parity, gx, [offs[0], offs[1], offs[2]])
         t_hi, t_lo = halves(both)
-        return both, mm3(t_hi, t_lo, f_hi, f_lo)
-
-    def mine_step(i, carry):
-        both, p = own_table(i)
-        tf[i, :, 0:ATOMS] = both
-        part[i, :, :, 0:CH] = p[0:64].reshape(8, 8, CH)
-        part[i, :, :, CH:2 * CH] = p[64:128].reshape(8, 8, CH)
+        p = mm3(t_hi, t_lo, f_hi, f_lo)
+        into[i, :, :, 0:CH] = p[0:64].reshape(8, 8, CH)
+        into[i, :, :, CH:2 * CH] = p[64:128].reshape(8, 8, CH)
+        return both
+
+    def own_step(i, carry):
+        own_table(i, 1, theirs)
+        tf[i, :, 0:ATOMS] = own_table(i, 0, part)
         return carry
 
-    def theirs_step(i, carry):
-        _, p = own_table(i + 4)
-        theirs[i, :, :, 0:CH] = p[0:64].reshape(8, 8, CH)
-        theirs[i, :, :, CH:2 * CH] = p[64:128].reshape(8, 8, CH)
-        return carry
-
-    lax.fori_loop(0, 4, theirs_step, 0)
-    lax.fori_loop(0, 4, mine_step, 0)
+    lax.fori_loop(0, 4, own_step, 0)
 
     sends = []
 
@@ -170,6 +183,9 @@
         pl.semaphore_signal(ready, inc=1, device_id=(column(k), gy), device_id_type=MESH)
     for q in range(2):
         start(theirs.at[pl.ds(2 * q, 2)], got0.at[pl.ds(2 * q, 2)], s_pair, r_pair, q, peer, gy)
+
+    for i, (x, y, slot) in enumerate(around):
+        start(near_pos.at[4], near_pos.at[slot], s_pos, r_pos, i, x, y)
 
     for q in range(2):
         arrived(got0.at[pl.ds(2 * q, 2)], r_pair, q)
@@ -178,15 +194,9 @@
             to = plane(k)
             start(part.at[2 * q + to // 8, lax.rem(to, 8)], got1.at[q, k], s_rs1, r_rs1, 16 * q + k, gx, to)
 
-    for load in loads[3:5]:
-        load.wait()
+    loads[4].wait()
     vw_hi, vw_lo = halves(vw[...])
-    halo[4, 0:CH, :] = jnp.transpose(mm3(f_hi, f_lo, vw_hi, vw_lo))
-    halo[4, CH:CH + 8, :] = jnp.zeros((8, ATOMS), F32)
-    for i in range(3):
-        halo[4, CH + i:CH + i + 1, :] = offs[i]
-    halo[4, CH + 3:CH + 4, :] = spec[0].astype(F32)
-    start(halo.at[4, pl.ds(CH, 8)], carry2, s_pair, r_pair, 2, peer, gy)
+    halo[4] = jnp.transpose(mm3(f_hi, f_lo, vw_hi, vw_lo))
     start(halo.at[4], halo.at[7 - 6 * c], s_halo, r_halo, 1, other, gy)
     start(halo.at[4], halo.at[1 + 6 * c], s_halo, r_halo, 0, peer, gy)
     pl.semaphore_wait(ready, 2)
@@ -220,10 +230,12 @@
     gf_hi, gf_lo = halves(gf[...])
     rows16[...] = jnp.zeros(rows16.shape, F32)
 
-    arrived(carry2, r_pair, 2)
+    for i, slot in enumerate(slots_here):
+        arrived(near_pos.at[slot], r_pos, i)
 
     def peer_step(i, carry):
-        tf[i, :, ATOMS:2 * ATOMS] = table(i, peer, [carry2[0:1], carry2[1:2], carry2[2:3]])
+        there = near_pos[from_peer + 1]
+        tf[i, :, ATOMS:2 * ATOMS] = table(i, 0, peer, [there[0:1], there[1:2], there[2:3]])
         return carry
 
     lax.fori_loop(0, 4, peer_step, 0)
@@ -258,6 +270,44 @@
 
     lax.fori_loop(0, SLOTS, onehot_step, 0)
 
+    found = [jnp.zeros((SLOTS, ATOMS), F32) for _ in range(4)]
+    for j in range(9):
+        for i in range(4):
+            row = jnp.broadcast_to(near_pos[j, i:i + 1, :], (SLOTS, ATOMS))
+            taken = jnp.take_along_axis(row, atom, axis=1)
+            found[i] = jnp.where(near == j, taken, found[i])
+    own = near_pos[4]
+    gap0 = (s.astype(F32) + found[0]) - own[0:1, :]
+    gap1 = (t.astype(F32) + found[1]) - own[1:2, :]
+    gap2 = found[2] - own[2:3, :]
+    dist[...] = jnp.sqrt(gap0 * gap0 + gap1 * gap1 + gap2 * gap2 + 0.01)
+    spj[...] = found[3]
+    own_kind = own[3:4, :]
+
+    def basis_step(e, carry):
+        lanes = pl.ds(pl.multiple_of(e * ATOMS, ATOMS), ATOMS)
+        k = lax.broadcasted_iota(jnp.int32, (RADIAL, ATOMS), 0).astype(F32)
+        scaled = (dist[pl.ds(e, 1), :] - k * (3.0 / 63)) / (6.0 / 63)
+        hi, lo = halves(jnp.exp(-scaled * scaled))
+        kinds = jnp.where(k == spj[pl.ds(e, 1), :], 1.0, 0.0) + jnp.where(k == own_kind, 1.0, 0.0)
+        kinds = kinds.astype(BF16)
+        bh[0:64, lanes] = hi
+        bh[64:128, lanes] = kinds
+        bh[128:192, lanes] = hi
+        bh[192:256, lanes] = kinds
+        bl[:, lanes] = lo
+        return carry
+
+    lax.fori_loop(0, SLOTS, basis_step, 0)
+
+    def filter_step(e, carry):
+        lanes = pl.ds(pl.multiple_of(e * 256, 256), 256)
+        before = mm(wcat[...], bh[:, lanes]) + mm(wcat[:, 0:64], bl[:, lanes])
+        hi, lo = halves(before / (1.0 + jnp.exp(-before)))
+        filt[:, lanes] = mm3(mix_hi[...], mix_lo[...], hi, lo)
+        return carry
+
+    lax.fori_loop(0, 4, filter_step, 0)
     total = sums[12]
     for k in (1, 15, 2, 14, 3, 13, 4, 12, 5, 11, 6, 10, 7, 9, 8):
         arrived(got2.at[k], r_rs2, k)
@@ -272,47 +322,6 @@
         at = (12 - d) % 16
         start(filt1.at[12], filt1.at[at], s_ag1, r_ag1, at, column(d), gy)
 
-    for i in range(3):
-        arrived(halo.at[3 * i], r_halo, 2 + i)
-        arrived(halo.at[3 * i + 2], r_halo, 5 + i)
-    found = [jnp.zeros((SLOTS, ATOMS), F32) for _ in range(4)]
-    for j in range(9):
-        for i in range(4):
-            row = jnp.broadcast_to(halo[j, CH + i:CH + i + 1, :], (SLOTS, ATOMS))
-            taken = jnp.take_along_axis(row, atom, axis=1)
-            found[i] = jnp.where(near == j, taken, found[i])
-    own = halo[4, CH:CH + 8, :]
-    gap0 = (s.astype(F32) + found[0]) - own[0:1, :]
-    gap1 = (t.astype(F32) + found[1]) - own[1:2, :]
-    gap2 = found[2] - own[2:3, :]
-    dist[...] = jnp.sqrt(gap0 * gap0 + gap1 * gap1 + gap2 * gap2 + 0.01)
-    spj[...] = found[3]
-    own_kind = own[3:4, :]
-
-    def basis_step(e, carry):
-        lanes = pl.ds(pl.multiple_of(e * ATOMS, ATOMS), ATOMS)
-        k = lax.broadcasted_iota(jnp.int32, (RADIAL, ATOMS), 0).astype(F32)
-        scaled = (dist[pl.ds(e, 1), :] - k * (3.0 / 63)) / (6.0 / 63)
-        hi, lo = halves(jnp.exp(-scaled * scaled))
-        kinds = jnp.where(k == spj[pl.ds(e, 1), :], 1.0, 0.0) + jnp.where(k == own_kind, 1.0, 0.0)
-        kinds = kinds.astype(BF16)
-        bh[0:64, lanes] = hi
-        bh[64:128, lanes] = kinds
-        bh[128:192, lanes] = hi
-        bh[192:256, lanes] = kinds
-        bl[:, lanes] = lo
-        return carry
-
-    lax.fori_loop(0, SLOTS, basis_step, 0)
-
-    def filter_step(e, carry):
-        lanes = pl.ds(pl.multiple_of(e * 256, 256), 256)
-        before = mm(wcat[...], bh[:, lanes]) + mm(wcat[:, 0:64], bl[:, lanes])
-        hi, lo = halves(before / (1.0 + jnp.exp(-before)))
-        filt[:, lanes] = mm3(mix_hi[...], mix_lo[...], hi, lo)
-        return carry
-
-    lax.fori_loop(0, 4, filter_step, 0)
     drain()
 
     def spread(q):
@@ -328,8 +337,11 @@
     spread(1)
     spread(0)
 
+    for i in range(3):
+        arrived(halo.at[3 * i], r_halo, 2 + i)
+        arrived(halo.at[3 * i + 2], r_halo, 5 + i)
     for j in range(9):
-        hi, lo = halves(halo[j, 0:CH, :])
+        hi, lo = halves(halo[j])
         vb[0:CH, ATOMS * j:ATOMS * j + ATOMS] = hi
         vb[CH:2 * CH, ATOMS * j:ATOMS * j + ATOMS] = lo
 
@@ -384,12 +396,12 @@
         pltpu.VMEM((2 * RADIAL, CH), F32),
         pltpu.VMEM((CH, CH), F32),
         pltpu.VMEM((CH, CH), F32),
-        pltpu.VMEM((8, ATOMS), F32),
-        pltpu.VMEM((9, CH + 8, ATOMS), F32),
+        pltpu.VMEM((9, 8, ATOMS), F32),
+        pltpu.VMEM((9, CH, ATOMS), F32),
         pltpu.VMEM((4, 128, 2 * ATOMS), F32),
         pltpu.VMEM((2, 2 * ATOMS, 256), BF16),
         pltpu.VMEM((2, 2 * ATOMS, 256), BF16),
-        pltpu.VMEM((MODES, 128), F32),
+        pltpu.VMEM((256, 128), F32),
         pltpu.VMEM((128, MODES), F32),
         pltpu.VMEM((4, 8, 8, 2 * CH), F32),
         pltpu.VMEM((4, 8, 8, 2 * CH), F32),
@@ -421,6 +433,7 @@
         dma((11,)),
         dma((4,)), dma((4,)),
         dma((8,)), dma((8,)),
+        dma((8,)), dma((8,)),
         dma((32,)), dma((32,)),
         dma((16,)), dma((16,)),
         dma((16,)), dma((16,)),

time: 54.2 us -> 49.2 us (0.908)
  Pallas kernels: 52.5 us -> 47.5 us
    pallas_call x1, Pallas kernels: 52.5 us -> 47.5 us  [shards(): pl.pallas_call(kernel, out_shape=jax.ShapeDtypeStruct((1, 1, ATOMS, CH),...]
where the time goes in v3:
time: 49.2 us; the launch traced here: 49 us
  Pallas kernels  47.5 us (97%)
  local copies, waits for them, and re-layouts  1.57 us (3%)
    pallas_call x1, Pallas kernels, shards(): pl.pallas_call(kernel, out_shape=jax.ShapeDtypeStruct((1, 1, ATOMS, CH),...  47.5 us
    unnamed x1, local copies, waits for them, and re-layouts  1.57 us

profile of v3, /device:TPU:1, one launch (start us, length us, event | category | flops | bytes accessed | tf_op | source)
XLA Modules:
  0.0 49.0 jit_solution(6789122712459715744)
XLA Ops:
  0.0 47.5 %shard_map.109 = f32[1,1,128,256]{3,2,1,0:T(8,128)} custom-call(f32[1,1,128,256]{3,2,1,0:T(8,128)} %feat_h.1, f32[1,3,1,128]{3,2,1,0:T(1,128)} %bitcast.5, s32[1,1,128]{2,1,0:T(1,128)} %spec_h.1, s32[1,1,8,128]{3,2,1,0:T(8,128)} %bitcast.3, s32[1,1,8,128]{3,2,1,0:T(8,128)} %bitcast.4, s32[3,512]{1,0:T(4,128)} %wv_h.1, f32[256,256]{1,0:T(8,128)} %vw_h.1, ...), custom_call_target="tpu_custom_call" | custom-call | tf_op jit(solution)/shard_map/pallas_call | solution.py:442
  47.5 1.6 %copy.13 = f32[1,1,128,256]{3,2,1,0:T(8,128)} copy(f32[1,1,128,256]{3,2,1,0:T(8,128)} %shard_map.109) | data formatting | bytes 262144

commit v4 on v3

--- a/solution.py
+++ b/solution.py
@@ -25,7 +25,9 @@
 PLANE_ORDER = (10, 9, 11, 6, 14, 8, 2, 5, 7, 13, 15, 4, 12, 1, 3)
 
 COS_TERMS = [(-1.0) ** n * TURN ** (2 * n) / math.factorial(2 * n) for n in range(7)]
-SIN_TERMS = [(-1.0) ** n * TURN ** (2 * n + 1) / math.factorial(2 * n + 1) for n in range(7)]
+
+DISTANCES = [8 + 2 * q + k if k < 2 else 4 - 2 * q + k for q in range(4) for k in range(4)]
+PLACE = [DISTANCES.index(d) for d in range(16)]
 
 
 def halves(x):
@@ -41,18 +43,15 @@
     return mm(a_hi, b_hi) + (mm(a_hi, b_lo) + mm(a_lo, b_hi))
 
 
-def cos_sin(turns):
-    q = jnp.floor(turns * 2.0 + 0.5)
-    r = turns - q * 0.5
-    h = q * 0.5
+def cos_turns(turns):
+    h = jnp.floor(turns * 2.0 + 0.5) * 0.5
+    r = turns - h
     sign = 1.0 - 4.0 * (h - jnp.floor(h))
     y = r * r
     c = jnp.full_like(y, COS_TERMS[6])
-    s = jnp.full_like(y, SIN_TERMS[6])
     for n in range(5, -1, -1):
         c = c * y + COS_TERMS[n]
-        s = s * y + SIN_TERMS[n]
-    return c * sign, s * (r * sign)
+    return c * sign
 
 
 def remote(src, dst, send, recv, gx, gy):
@@ -66,7 +65,7 @@
     out,
     feat, offs, spec, neigh, mask, wv, vw, embed, mixw, gf,
     near_pos, halo, tf, tt_hi, tt_lo, ncol, wpad,
-    part, theirs, got0, got1, sums, got2, rows16, filt1, filt2, filt3, rh_hi, rh_lo, lsum, lpeer, lgot,
+    part, theirs, got0, got1, sums, got2, rows16, own_row, filt1, filt2, filt3, rh_hi, rh_lo, lsum, lpeer, lgot,
     dist, spj, rowid, onehot, bh, bl, filt, wcat, mix_hi, mix_lo, vb,
     ready, s_in, s_pair, r_pair, s_pos, r_pos, s_halo, r_halo, s_rs1, r_rs1, s_rs2, r_rs2, s_ag1, r_ag1, s_ag2, r_ag2,
 ):
@@ -129,32 +128,36 @@
     odd = pltpu.roll(even, MODES - 16, 1)
     wpad[0:8, :] = jnp.where(c == 0, even, odd)
     wpad[8:16, :] = jnp.where(c == 0, odd, even)
-    r = lax.broadcasted_iota(jnp.int32, (256, 1), 0)
-    m = lax.broadcasted_iota(jnp.int32, (256, MODES), 1)
-    target = 32 * ((z + 4 + 8 * (r >> 7) + (r & 7)) & 15) + ((r >> 3) & 15)
+    r = lax.broadcasted_iota(jnp.int32, (MODES, 1), 0)
+    m = lax.broadcasted_iota(jnp.int32, (MODES, MODES), 1)
+    q, k = r >> 7, r & 3
+    away = jnp.where(k < 2, 8 + 2 * q, 4 - 2 * q) + k
+    target = 32 * ((z + away) & 15) + ((r >> 3) & 15)
     pick = jnp.where(m == target, 1.0, 0.0).astype(BF16)
     ncol[...] = lax.dot_general(
         pick, wpad[...].astype(BF16), (((1,), (1,)), ((), ())), preferred_element_type=F32
     )
 
     def table(i, parity, block, positions):
-        n = ncol[pl.ds(pl.multiple_of(i * 64, 64), 64), :]
-        n0, n1, n2 = [n[:, 8 * parity + a:8 * parity + a + 1] for a in range(3)]
-        w0 = (n0.astype(jnp.int32) * block & 31).astype(F32)
-        w1 = (n1.astype(jnp.int32) * gy & 15).astype(F32)
-        turns = (w0 + n0 * positions[0]) * (1.0 / 32)
-        turns = turns + (w1 + n1 * positions[1]) * (1.0 / 16)
-        turns = turns + n2 * positions[2]
-        return jnp.concatenate(cos_sin(turns), axis=0)
+        quarter = ((lax.broadcasted_iota(jnp.int32, (64, ATOMS), 0) >> 2) & 1).astype(F32) * 0.25
+        rows = []
+        for h in range(2):
+            n = ncol[pl.ds(pl.multiple_of(i * 128 + h * 64, 64), 64), :]
+            n0, n1, n2 = [n[:, 8 * parity + a:8 * parity + a + 1] for a in range(3)]
+            w0 = (n0.astype(jnp.int32) * block & 31).astype(F32)
+            w1 = (n1.astype(jnp.int32) * gy & 15).astype(F32)
+            turns = (w0 + n0 * positions[0]) * (1.0 / 32)
+            turns = turns + (w1 + n1 * positions[1]) * (1.0 / 16)
+            turns = turns + n2 * positions[2]
+            rows.append(cos_turns(turns - quarter))
+        return jnp.concatenate(rows, axis=0)
 
     f_hi, f_lo = halves(feat[...])
 
     def own_table(i, parity, into):
         both = table(i, parity, gx, [offs[0], offs[1], offs[2]])
         t_hi, t_lo = halves(both)
-        p = mm3(t_hi, t_lo, f_hi, f_lo)
-        into[i, :, :, 0:CH] = p[0:64].reshape(8, 8, CH)
-        into[i, :, :, CH:2 * CH] = p[64:128].reshape(8, 8, CH)
+        into[i] = mm3(t_hi, t_lo, f_hi, f_lo).reshape(16, 8, CH)
         return both
 
     def own_step(i, carry):
@@ -171,28 +174,32 @@
         copy.start()
         sends.append(copy)
 
+    def start_all(copies, s_sems, r_sems, i, whole):
+        for src, dst, x, y in copies:
+            remote(src, dst, s_sems.at[i], r_sems.at[i], x, y).start()
+        sends.append(remote(whole, whole, s_sems.at[i], r_sems.at[i], peer, gy))
+
     def arrived(dst, r_sems, i):
         remote(dst, dst, s_pair.at[0], r_sems.at[i], peer, gy).wait_recv()
 
     def drain():
         while sends:
-            sends.pop().wait_send()
+            sends.pop(0).wait_send()
 
     pl.semaphore_wait(barrier, len(greeted))
     for k in (4, 12):
         pl.semaphore_signal(ready, inc=1, device_id=(column(k), gy), device_id_type=MESH)
-    for q in range(2):
-        start(theirs.at[pl.ds(2 * q, 2)], got0.at[pl.ds(2 * q, 2)], s_pair, r_pair, q, peer, gy)
+    for q in range(4):
+        start(theirs.at[q], got0.at[q], s_pair, r_pair, q, peer, gy)
 
     for i, (x, y, slot) in enumerate(around):
         start(near_pos.at[4], near_pos.at[slot], s_pos, r_pos, i, x, y)
 
-    for q in range(2):
-        arrived(got0.at[pl.ds(2 * q, 2)], r_pair, q)
-        part[2 * q:2 * q + 2] = part[2 * q:2 * q + 2] + got0[2 * q:2 * q + 2]
-        for k in PLANE_ORDER:
-            to = plane(k)
-            start(part.at[2 * q + to // 8, lax.rem(to, 8)], got1.at[q, k], s_rs1, r_rs1, 16 * q + k, gx, to)
+    for q in range(4):
+        arrived(got0.at[q], r_pair, q)
+        part[q] = part[q] + got0[q]
+        copies = [(part.at[q, plane(k)], got1.at[q, k], gx, plane(k)) for k in PLANE_ORDER]
+        start_all(copies, s_rs1, r_rs1, q, got1.at[q, pl.ds(1, 15)])
 
     loads[4].wait()
     vw_hi, vw_lo = halves(vw[...])
@@ -201,17 +208,22 @@
     start(halo.at[4], halo.at[1 + 6 * c], s_halo, r_halo, 0, peer, gy)
     pl.semaphore_wait(ready, 2)
 
-    for q in range(2):
-        total = part[2 * q + gy // 8, lax.rem(gy, 8)]
+    copies = []
+    for q in range(4):
+        arrived(got1.at[q, pl.ds(1, 15)], r_rs1, q)
+        total = part[q, gy]
         for k in range(1, 16):
-            arrived(got1.at[q, k], r_rs1, 16 * q + k)
             total = total + got1[q, k]
-        for k in range(8):
-            sums[8 * q + k] = total[k:k + 1, :]
-        for k in (4, 3, 5, 2, 6, 1, 7, 0):
-            d = (4 + 8 * q + k) % 16
+        for k in range(4):
+            sums[4 * q + k, 0:1, :] = total[k:k + 1, :]
+            sums[4 * q + k, 1:2, :] = total[4 + k:5 + k, :]
+        for k in (0, 1, 3, 2):
+            d = DISTANCES[4 * q + k]
             if d:
-                start(sums.at[8 * q + k], got2.at[d], s_rs2, r_rs2, d, column(d), gy)
+                remote(
+                    sums.at[4 * q + k], got2.at[d], s_rs2.at[0], r_rs2.at[0], column(d), gy
+                ).start()
+    sends.append(remote(got2.at[pl.ds(1, 15)], got2.at[pl.ds(1, 15)], s_rs2.at[0], r_rs2.at[0], peer, gy))
 
     arrived(halo.at[7 - 6 * c], r_halo, 0)
     arrived(halo.at[1 + 6 * c], r_halo, 1)
@@ -241,8 +253,8 @@
     lax.fori_loop(0, 4, peer_step, 0)
     for i in range(4):
         hi, lo = halves(jnp.transpose(tf[i]))
-        tt_hi[i // 2, :, 128 * (i % 2):128 * (i % 2) + 128] = hi
-        tt_lo[i // 2, :, 128 * (i % 2):128 * (i % 2) + 128] = lo
+        tt_hi[i] = hi
+        tt_lo[i] = lo
     wt = jnp.transpose(embed[...])
     hi, lo = halves(wt)
     wcat[:, 0:128] = hi
@@ -308,34 +320,31 @@
         return carry
 
     lax.fori_loop(0, 4, filter_step, 0)
-    total = sums[12]
-    for k in (1, 15, 2, 14, 3, 13, 4, 12, 5, 11, 6, 10, 7, 9, 8):
-        arrived(got2.at[k], r_rs2, k)
+    arrived(got2.at[pl.ds(1, 15)], r_rs2, 0)
+    total = sums[PLACE[0]]
+    for k in range(1, 16):
         total = total + got2[k]
-    rows16[0:1, :] = total[:, 0:CH]
-    rows16[1:2, :] = total[:, CH:2 * CH]
+    rows16[0:2, :] = total
     a_hi, a_lo = halves(rows16[...])
     mixed = mm3(a_hi, a_lo, gf_hi, gf_lo)
-    filt1[12, :, 0:CH] = mixed[0:1, :] * damp
-    filt1[12, :, CH:2 * CH] = mixed[1:2, :] * damp
+    own_row[0] = mixed[0:2, :] * damp
     for d in (8, 7, 9, 6, 10, 5, 11, 4, 12, 3, 13, 2, 14, 1, 15):
-        at = (12 - d) % 16
-        start(filt1.at[12], filt1.at[at], s_ag1, r_ag1, at, column(d), gy)
+        at = PLACE[16 - d]
+        remote(own_row.at[0], filt1.at[at], s_ag1.at[0], r_ag1.at[at // 4], column(d), gy).start()
+    sends.append(remote(got2.at[pl.ds(1, 15)], got2.at[pl.ds(1, 15)], s_ag1.at[0], r_ag1.at[0], peer, gy))
 
     drain()
 
-    def spread(q):
-        for k in range(8):
-            at = 8 * q + k
-            if at != 12:
-                arrived(filt1.at[at], r_ag1, at)
-            filt2[q, k:k + 1, :] = filt1[at]
-        for k in PLANE_ORDER:
-            start(filt2.at[q], filt3.at[q, gy], s_ag2, r_ag2, 16 * q + k, gx, plane(k))
+    for q in (3, 2, 1, 0):
+        arrived(filt1.at[pl.ds(4 * q, 4 if q < 3 else 3)], r_ag1, q)
+        for k in range(4):
+            at = 4 * q + k
+            row = own_row.at[0] if at == PLACE[0] else filt1.at[at]
+            filt2[q, k:k + 1, :] = row[0:1, :]
+            filt2[q, 4 + k:5 + k, :] = row[1:2, :]
+        copies = [(filt2.at[q], filt3.at[q, gy], gx, plane(k)) for k in PLANE_ORDER]
+        start_all(copies, s_ag2, r_ag2, q, got1.at[q, pl.ds(1, 15)])
         filt3[q, gy] = filt2[q]
-
-    spread(1)
-    spread(0)
 
     for i in range(3):
         arrived(halo.at[3 * i], r_halo, 2 + i)
@@ -355,28 +364,25 @@
     out[0, 0] = jnp.transpose(short) * (1.0 / math.sqrt(SLOTS))
 
     def factors(q):
-        for k in range(1, 16):
-            sender = lax.rem(px + 4 - k // 4, 4) * 4 + lax.rem(py + 4 - k % 4, 4)
-            arrived(filt3.at[q, sender], r_ag2, 16 * q + k)
-        for h in range(2):
-            hi, lo = halves(filt3[q, 8 * h:8 * h + 8].reshape(64, 2 * CH))
-            for at, lane in ((128 * h, 0), (128 * h + 64, CH)):
-                rh_hi[at:at + 64, :] = hi[:, lane:lane + CH]
-                rh_lo[at:at + 64, :] = lo[:, lane:lane + CH]
+        arrived(filt3.at[q, pl.ds(0, 15)], r_ag2, q)
+        hi, lo = halves(filt3[q].reshape(128, CH))
+        rh_hi[...] = hi
+        rh_lo[...] = lo
 
     def terms(q, rows):
         return mm3(tt_hi[q, rows], tt_lo[q, rows], rh_hi[...], rh_lo[...])
 
     near_rows, far_rows = slice(0, ATOMS), slice(ATOMS, 2 * ATOMS)
-    factors(1)
-    lsum[...] = terms(1, far_rows)
-    out[0, 0] += terms(1, near_rows)
+    for q in (3, 2, 1):
+        factors(q)
+        lsum[...] = terms(q, far_rows) + (lsum[...] if q < 3 else 0.0)
+        out[0, 0] += terms(q, near_rows)
     drain()
     factors(0)
     lpeer[...] = lsum[...] + terms(0, far_rows)
-    start(lpeer, lgot, s_pair, r_pair, 3, peer, gy)
+    start(lpeer, lgot, s_pair, r_pair, 4, peer, gy)
     base = out[0, 0] + terms(0, near_rows)
-    arrived(lgot, r_pair, 3)
+    arrived(lgot, r_pair, 4)
     out[0, 0] = base + lgot[...]
     drain()
 
@@ -399,22 +405,23 @@
         pltpu.VMEM((9, 8, ATOMS), F32),
         pltpu.VMEM((9, CH, ATOMS), F32),
         pltpu.VMEM((4, 128, 2 * ATOMS), F32),
-        pltpu.VMEM((2, 2 * ATOMS, 256), BF16),
-        pltpu.VMEM((2, 2 * ATOMS, 256), BF16),
-        pltpu.VMEM((256, 128), F32),
+        pltpu.VMEM((4, 2 * ATOMS, 128), BF16),
+        pltpu.VMEM((4, 2 * ATOMS, 128), BF16),
+        pltpu.VMEM((MODES, 128), F32),
         pltpu.VMEM((128, MODES), F32),
-        pltpu.VMEM((4, 8, 8, 2 * CH), F32),
-        pltpu.VMEM((4, 8, 8, 2 * CH), F32),
-        pltpu.VMEM((4, 8, 8, 2 * CH), F32),
-        pltpu.VMEM((2, GY, 8, 2 * CH), F32),
-        pltpu.VMEM((NZ, 1, 2 * CH), F32),
-        pltpu.VMEM((NZ, 1, 2 * CH), F32),
+        pltpu.VMEM((4, GY, 8, CH), F32),
+        pltpu.VMEM((4, GY, 8, CH), F32),
+        pltpu.VMEM((4, GY, 8, CH), F32),
+        pltpu.VMEM((4, GY, 8, CH), F32),
+        pltpu.VMEM((NZ, 2, CH), F32),
+        pltpu.VMEM((NZ, 2, CH), F32),
         pltpu.VMEM((16, CH), F32),
-        pltpu.VMEM((NZ, 1, 2 * CH), F32),
-        pltpu.VMEM((2, 8, 2 * CH), F32),
-        pltpu.VMEM((2, GY, 8, 2 * CH), F32),
-        pltpu.VMEM((256, CH), BF16),
-        pltpu.VMEM((256, CH), BF16),
+        pltpu.VMEM((1, 2, CH), F32),
+        pltpu.VMEM((NZ, 2, CH), F32),
+        pltpu.VMEM((4, 8, CH), F32),
+        pltpu.VMEM((4, GY, 8, CH), F32),
+        pltpu.VMEM((128, CH), BF16),
+        pltpu.VMEM((128, CH), BF16),
         pltpu.VMEM((ATOMS, CH), F32),
         pltpu.VMEM((ATOMS, CH), F32),
         pltpu.VMEM((ATOMS, CH), F32),
@@ -431,13 +438,13 @@
         pltpu.VMEM((2 * CH, 9 * ATOMS), BF16),
         pltpu.SemaphoreType.REGULAR,
         dma((11,)),
-        dma((4,)), dma((4,)),
+        dma((5,)), dma((5,)),
         dma((8,)), dma((8,)),
         dma((8,)), dma((8,)),
-        dma((32,)), dma((32,)),
-        dma((16,)), dma((16,)),
-        dma((16,)), dma((16,)),
-        dma((32,)), dma((32,)),
+        dma((4,)), dma((4,)),
+        dma((1,)), dma((1,)),
+        dma((1,)), dma((4,)),
+        dma((4,)), dma((4,)),
     ]
     return pl.pallas_call(
         kernel,

time: 49.2 us -> 47.6 us (0.967)
  Pallas kernels: 47.5 us -> 45.9 us
    pallas_call x1, Pallas kernels: 47.5 us -> 45.9 us  [shards(): pl.pallas_call(kernel, out_shape=jax.ShapeDtypeStruct((1, 1, ATOMS, CH),...]
where the time goes in v4:
time: 47.6 us; the launch traced here: 47.5 us
  Pallas kernels  45.9 us (96%)
  local copies, waits for them, and re-layouts  1.57 us (3%)
    pallas_call x1, Pallas kernels, shards(): pl.pallas_call(kernel, out_shape=jax.ShapeDtypeStruct((1, 1, ATOMS, CH),...  45.9 us
    unnamed x1, local copies, waits for them, and re-layouts  1.57 us

profile of v4, /device:TPU:1, one launch (start us, length us, event | category | flops | bytes accessed | tf_op | source)
XLA Modules:
  0.0 47.5 jit_solution(17900899397326530458)
XLA Ops:
  0.0 45.9 %shard_map.109 = f32[1,1,128,256]{3,2,1,0:T(8,128)} custom-call(f32[1,1,128,256]{3,2,1,0:T(8,128)} %feat_h.1, f32[1,3,1,128]{3,2,1,0:T(1,128)} %bitcast.5, s32[1,1,128]{2,1,0:T(1,128)} %spec_h.1, s32[1,1,8,128]{3,2,1,0:T(8,128)} %bitcast.3, s32[1,1,8,128]{3,2,1,0:T(8,128)} %bitcast.4, s32[3,512]{1,0:T(4,128)} %wv_h.1, f32[256,256]{1,0:T(8,128)} %vw_h.1, ...), custom_call_target="tpu_custom_call" | custom-call | tf_op jit(solution)/shard_map/pallas_call | solution.py:449
  45.9 1.6 %copy.13 = f32[1,1,128,256]{3,2,1,0:T(8,128)} copy(f32[1,1,128,256]{3,2,1,0:T(8,128)} %shard_map.109) | data formatting | bytes 262144

commit v5 on v4

--- a/solution.py
+++ b/solution.py
@@ -54,6 +54,12 @@
     return c * sign
 
 
+def stacked(hi_lo, b_hi, b_lo):
+    rows = hi_lo.shape[0] // 2
+    upper = mm(hi_lo, b_hi)
+    return upper[0:rows] + (upper[rows:] + mm(hi_lo[0:rows], b_lo))
+
+
 def remote(src, dst, send, recv, gx, gy):
     return pltpu.make_async_remote_copy(
         src_ref=src, dst_ref=dst, send_sem=send, recv_sem=recv, device_id=(gx, gy), device_id_type=MESH
@@ -64,7 +70,7 @@
     feat_h, offs_h, spec_h, neigh_h, mask_h, wv_h, vw_h, radw_h, emb_h, mixw_h, gf_h,
     out,
     feat, offs, spec, neigh, mask, wv, vw, embed, mixw, gf,
-    near_pos, halo, tf, tt_hi, tt_lo, ncol, wpad,
+    near_pos, halo, tf, tt, ncol, wpad,
     part, theirs, got0, got1, sums, got2, rows16, own_row, filt1, filt2, filt3, rh_hi, rh_lo, lsum, lpeer, lgot,
     dist, spj, rowid, onehot, bh, bl, filt, wcat, mix_hi, mix_lo, vb,
     ready, s_in, s_pair, r_pair, s_pos, r_pos, s_halo, r_halo, s_rs1, r_rs1, s_rs2, r_rs2, s_ag1, r_ag1, s_ag2, r_ag2,
@@ -98,9 +104,12 @@
     ]
 
     barrier = pltpu.get_barrier_semaphore()
-    greeted = [(column(k), gy) for k in (4, 12, 3, 13, 2, 14, 1, 15)]
-    greeted += [(gx, plane(k)) for k in PLANE_ORDER]
-    greeted += [(other, up), (other, down), (peer, up), (peer, down), (other, gy), (peer, gy)]
+    greeted = [(gx, plane(10)), (column(4), gy), (column(12), gy)]
+    greeted += [(gx, plane(k)) for k in PLANE_ORDER[1:5]] + [(other, up), (other, down)]
+    greeted += [(column(3), gy), (column(13), gy), (peer, up), (peer, down)]
+    greeted += [(gx, plane(k)) for k in PLANE_ORDER[5:11]] + [(column(2), gy), (column(14), gy)]
+    greeted += [(gx, plane(k)) for k in PLANE_ORDER[11:]] + [(column(1), gy), (column(15), gy)]
+    greeted += [(other, gy), (peer, gy)]
     for device in greeted:
         pl.semaphore_signal(barrier, inc=1, device_id=device, device_id_type=MESH)
 
@@ -253,8 +262,9 @@
     lax.fori_loop(0, 4, peer_step, 0)
     for i in range(4):
         hi, lo = halves(jnp.transpose(tf[i]))
-        tt_hi[i] = hi
-        tt_lo[i] = lo
+        for at, rows in ((0, slice(ATOMS, 2 * ATOMS)), (2 * ATOMS, slice(0, ATOMS))):
+            tt[i, at:at + ATOMS, :] = hi[rows]
+            tt[i, at + ATOMS:at + 2 * ATOMS, :] = lo[rows]
     wt = jnp.transpose(embed[...])
     hi, lo = halves(wt)
     wcat[:, 0:128] = hi
@@ -325,8 +335,7 @@
     for k in range(1, 16):
         total = total + got2[k]
     rows16[0:2, :] = total
-    a_hi, a_lo = halves(rows16[...])
-    mixed = mm3(a_hi, a_lo, gf_hi, gf_lo)
+    mixed = stacked(jnp.concatenate(halves(rows16[...]), axis=0), gf_hi, gf_lo)
     own_row[0] = mixed[0:2, :] * damp
     for d in (8, 7, 9, 6, 10, 5, 11, 4, 12, 3, 13, 2, 14, 1, 15):
         at = PLACE[16 - d]
@@ -370,9 +379,9 @@
         rh_lo[...] = lo
 
     def terms(q, rows):
-        return mm3(tt_hi[q, rows], tt_lo[q, rows], rh_hi[...], rh_lo[...])
-
-    near_rows, far_rows = slice(0, ATOMS), slice(ATOMS, 2 * ATOMS)
+        return stacked(tt[q, rows], rh_hi[...], rh_lo[...])
+
+    near_rows, far_rows = slice(2 * ATOMS, 4 * ATOMS), slice(0, 2 * ATOMS)
     for q in (3, 2, 1):
         factors(q)
         lsum[...] = terms(q, far_rows) + (lsum[...] if q < 3 else 0.0)
@@ -405,8 +414,7 @@
         pltpu.VMEM((9, 8, ATOMS), F32),
         pltpu.VMEM((9, CH, ATOMS), F32),
         pltpu.VMEM((4, 128, 2 * ATOMS), F32),
-        pltpu.VMEM((4, 2 * ATOMS, 128), BF16),
-        pltpu.VMEM((4, 2 * ATOMS, 128), BF16),
+        pltpu.VMEM((4, 4 * ATOMS, 128), BF16),
         pltpu.VMEM((MODES, 128), F32),
         pltpu.VMEM((128, MODES), F32),
         pltpu.VMEM((4, GY, 8, CH), F32),
@@ -453,12 +461,12 @@
         out_specs=vmem,
         scratch_shapes=scratch,
         compiler_params=pltpu.CompilerParams(
-            collective_id=0, has_side_effects=True, vmem_limit_bytes=56 * 1024 * 1024
+            collective_id=0, has_side_effects=True, vmem_limit_bytes=40 * 1024 * 1024
         ),
-    )(
+    )(*[pltpu.with_memory_space_constraint(x, pltpu.HBM) for x in (
         features, jnp.transpose(offsets, (0, 2, 1, 3)), species, jnp.swapaxes(neighbours, 2, 3),
         jnp.swapaxes(edge_mask, 2, 3), wavevectors, vw, radw, emb, mixw, gf,
-    )
+    )])
 
 
 def solution(mesh):

time: 47.6 us -> 46 us (0.966)
  local copies, waits for them, and re-layouts: 1.57 us -> 0.66 us
  Pallas kernels: 45.9 us -> 45.2 us
    unnamed x1, local copies, waits for them, and re-layouts: 1.57 us -> 0.66 us
    pallas_call x1, Pallas kernels: 45.9 us -> 45.2 us  [shards(): pl.pallas_call(kernel, out_shape=jax.ShapeDtypeStruct((1, 1, ATOMS, CH),...]
where the time goes in v5:
time: 46 us; the launch traced here: 45.9 us
  Pallas kernels  45.2 us (98%)
  local copies, waits for them, and re-layouts  0.66 us (1%)
    pallas_call x1, Pallas kernels, shards(): pl.pallas_call(kernel, out_shape=jax.ShapeDtypeStruct((1, 1, ATOMS, CH),...  45.2 us

profile of v5, /device:TPU:1, one launch (start us, length us, event | category | flops | bytes accessed | tf_op | source)
XLA Modules:
  0.0 45.9 jit_solution(17799964096382235502)
XLA Ops:
  0.0 45.2 %shard_map.109 = f32[1,1,128,256]{3,2,1,0:T(8,128)S(1)} custom-call(f32[1,1,128,256]{3,2,1,0:T(8,128)} %feat_h.1, f32[1,3,1,128]{3,2,1,0:T(1,128)} %bitcast.5, s32[1,1,128]{2,1,0:T(1,128)} %spec_h.1, s32[1,1,8,128]{3,2,1,0:T(8,128)} %bitcast.3, s32[1,1,8,128]{3,2,1,0:T(8,128)} %bitcast.4, s32[3,512]{1,0:T(4,128)} %wv_h.1, f32[256,256]{1,0:T(8,128)} %vw_h.1, ...), custom_call_target="tpu_custom_call" | custom-call | tf_op jit(solution)/shard_map/pallas_call | solution.py:457
  45.2 0.7 %copy.13 = f32[1,1,128,256]{3,2,1,0:T(8,128)} copy(f32[1,1,128,256]{3,2,1,0:T(8,128)S(1)} %shard_map.109) | data formatting | bytes 262144

commit v6 on v5

--- a/solution.py
+++ b/solution.py
@@ -71,9 +71,9 @@
     out,
     feat, offs, spec, neigh, mask, wv, vw, embed, mixw, gf,
     near_pos, halo, tf, tt, ncol, wpad,
-    part, theirs, got0, got1, sums, got2, rows16, own_row, filt1, filt2, filt3, rh_hi, rh_lo, lsum, lpeer, lgot,
+    part, theirs, got0, got1, sums, got2, rows16, own_row, filt1, filt2, filt3, rh_hi, rh_lo, lsum, lgot, last, tf_theirs, tt_theirs,
     dist, spj, rowid, onehot, bh, bl, filt, wcat, mix_hi, mix_lo, vb,
-    ready, s_in, s_pair, r_pair, s_pos, r_pos, s_halo, r_halo, s_rs1, r_rs1, s_rs2, r_rs2, s_ag1, r_ag1, s_ag2, r_ag2,
+    ready, s_in, s_pair, r_pair, s_pos, r_pos, s_halo, r_halo, s_rs1, r_rs1, s_rs2, r_rs2, s_ag1, r_ag1, s_ag2, r_ag2, s_last, r_last,
 ):
     gx = lax.axis_index("gx")
     gy = lax.axis_index("gy")
@@ -170,7 +170,7 @@
         return both
 
     def own_step(i, carry):
-        own_table(i, 1, theirs)
+        tf_theirs[i] = own_table(i, 1, theirs)
         tf[i, :, 0:ATOMS] = own_table(i, 0, part)
         return carry
 
@@ -196,11 +196,11 @@
             sends.pop(0).wait_send()
 
     pl.semaphore_wait(barrier, len(greeted))
+    for q in range(4):
+        start(theirs.at[q], got0.at[q], s_pair, r_pair, q, peer, gy)
+
     for k in (4, 12):
         pl.semaphore_signal(ready, inc=1, device_id=(column(k), gy), device_id_type=MESH)
-    for q in range(4):
-        start(theirs.at[q], got0.at[q], s_pair, r_pair, q, peer, gy)
-
     for i, (x, y, slot) in enumerate(around):
         start(near_pos.at[4], near_pos.at[slot], s_pos, r_pos, i, x, y)
 
@@ -265,6 +265,9 @@
         for at, rows in ((0, slice(ATOMS, 2 * ATOMS)), (2 * ATOMS, slice(0, ATOMS))):
             tt[i, at:at + ATOMS, :] = hi[rows]
             tt[i, at + ATOMS:at + 2 * ATOMS, :] = lo[rows]
+    hi, lo = halves(jnp.transpose(tf_theirs[0]))
+    tt_theirs[0:ATOMS] = hi
+    tt_theirs[ATOMS:2 * ATOMS] = lo
     wt = jnp.transpose(embed[...])
     hi, lo = halves(wt)
     wcat[:, 0:128] = hi
@@ -353,6 +356,9 @@
             filt2[q, 4 + k:5 + k, :] = row[1:2, :]
         copies = [(filt2.at[q], filt3.at[q, gy], gx, plane(k)) for k in PLANE_ORDER]
         start_all(copies, s_ag2, r_ag2, q, got1.at[q, pl.ds(1, 15)])
+        if q == 0:
+            copies = [(filt2.at[0], last.at[gy], peer, plane(k)) for k in PLANE_ORDER + (0,)]
+            start_all(copies, s_last, r_last, 0, got1.at[0])
         filt3[q, gy] = filt2[q]
 
     for i in range(3):
@@ -386,14 +392,15 @@
         factors(q)
         lsum[...] = terms(q, far_rows) + (lsum[...] if q < 3 else 0.0)
         out[0, 0] += terms(q, near_rows)
+    start(lsum, lgot, s_pair, r_pair, 4, peer, gy)
     drain()
+    arrived(lgot, r_pair, 4)
+    out[0, 0] += lgot[...]
     factors(0)
-    lpeer[...] = lsum[...] + terms(0, far_rows)
-    start(lpeer, lgot, s_pair, r_pair, 4, peer, gy)
-    base = out[0, 0] + terms(0, near_rows)
-    arrived(lgot, r_pair, 4)
-    out[0, 0] = base + lgot[...]
-    drain()
+    base = terms(0, near_rows)
+    arrived(last, r_last, 0)
+    hi, lo = halves(last[...].reshape(128, CH))
+    out[0, 0] += base + stacked(tt_theirs[...], hi, lo)
 
 
 def shards(features, offsets, species, neighbours, edge_mask, wavevectors, vw, radw, emb, mixw, gf):
@@ -432,7 +439,9 @@
         pltpu.VMEM((128, CH), BF16),
         pltpu.VMEM((ATOMS, CH), F32),
         pltpu.VMEM((ATOMS, CH), F32),
-        pltpu.VMEM((ATOMS, CH), F32),
+        pltpu.VMEM((GY, 8, CH), F32),
+        pltpu.VMEM((4, 128, ATOMS), F32),
+        pltpu.VMEM((2 * ATOMS, 128), BF16),
         pltpu.VMEM((SLOTS, ATOMS), F32),
         pltpu.VMEM((SLOTS, ATOMS), F32),
         pltpu.VMEM((SLOTS, ATOMS), jnp.int32),
@@ -453,6 +462,7 @@
         dma((1,)), dma((1,)),
         dma((1,)), dma((4,)),
         dma((4,)), dma((4,)),
+        dma((1,)), dma((1,)),
     ]
     return pl.pallas_call(
         kernel,

time: 46 us -> 45.9 us (level)
  no operation moved by 1% of the time
where the time goes in v6:
time: 45.9 us; the launch traced here: 45.8 us
  Pallas kernels  45.1 us (98%)
  local copies, waits for them, and re-layouts  0.66 us (1%)
    pallas_call x1, Pallas kernels, shards(): pl.pallas_call(kernel, out_shape=jax.ShapeDtypeStruct((1, 1, ATOMS, CH),...  45.1 us

profile of v6, /device:TPU:1, one launch (start us, length us, event | category | flops | bytes accessed | tf_op | source)
XLA Modules:
  0.0 45.8 jit_solution(18229691209397234932)
XLA Ops:
  0.0 45.1 %shard_map.109 = f32[1,1,128,256]{3,2,1,0:T(8,128)S(1)} custom-call(f32[1,1,128,256]{3,2,1,0:T(8,128)} %feat_h.1, f32[1,3,1,128]{3,2,1,0:T(1,128)} %bitcast.5, s32[1,1,128]{2,1,0:T(1,128)} %spec_h.1, s32[1,1,8,128]{3,2,1,0:T(8,128)} %bitcast.3, s32[1,1,8,128]{3,2,1,0:T(8,128)} %bitcast.4, s32[3,512]{1,0:T(4,128)} %wv_h.1, f32[256,256]{1,0:T(8,128)} %vw_h.1, ...), custom_call_target="tpu_custom_call" | custom-call | tf_op jit(solution)/shard_map/pallas_call | solution.py:467
  45.1 0.7 %copy.13 = f32[1,1,128,256]{3,2,1,0:T(8,128)} copy(f32[1,1,128,256]{3,2,1,0:T(8,128)S(1)} %shard_map.109) | data formatting | bytes 262144

commit v7 on v6

--- a/solution.py
+++ b/solution.py
@@ -354,11 +354,16 @@
             row = own_row.at[0] if at == PLACE[0] else filt1.at[at]
             filt2[q, k:k + 1, :] = row[0:1, :]
             filt2[q, 4 + k:5 + k, :] = row[1:2, :]
-        copies = [(filt2.at[q], filt3.at[q, gy], gx, plane(k)) for k in PLANE_ORDER]
-        start_all(copies, s_ag2, r_ag2, q, got1.at[q, pl.ds(1, 15)])
+        for k in PLANE_ORDER:
+            to = plane(k)
+            remote(filt2.at[q], filt3.at[q, gy], s_ag2.at[q], r_ag2.at[q], gx, to).start()
+            if q == 0:
+                remote(filt2.at[0], last.at[gy], s_last.at[0], r_last.at[0], peer, to).start()
         if q == 0:
-            copies = [(filt2.at[0], last.at[gy], peer, plane(k)) for k in PLANE_ORDER + (0,)]
-            start_all(copies, s_last, r_last, 0, got1.at[0])
+            remote(filt2.at[0], last.at[gy], s_last.at[0], r_last.at[0], peer, gy).start()
+            sends.append(remote(got1.at[0], got1.at[0], s_last.at[0], r_last.at[0], peer, gy))
+        whole = got1.at[q, pl.ds(1, 15)]
+        sends.append(remote(whole, whole, s_ag2.at[q], r_ag2.at[q], peer, gy))
         filt3[q, gy] = filt2[q]
 
     for i in range(3):

time: 45.9 us -> 46.2 us (level)
  no operation moved by 1% of the time
where the time goes in v7:
time: 46.2 us; the launch traced here: 46 us
  Pallas kernels  45.4 us (98%)
  local copies, waits for them, and re-layouts  0.66 us (1%)
    pallas_call x1, Pallas kernels, shards(): pl.pallas_call(kernel, out_shape=jax.ShapeDtypeStruct((1, 1, ATOMS, CH),...  45.4 us

profile of v7, /device:TPU:1, one launch (start us, length us, event | category | flops | bytes accessed | tf_op | source)
XLA Modules:
  0.0 46.0 jit_solution(5068194303362613993)
XLA Ops:
  0.0 45.4 %shard_map.109 = f32[1,1,128,256]{3,2,1,0:T(8,128)S(1)} custom-call(f32[1,1,128,256]{3,2,1,0:T(8,128)} %feat_h.1, f32[1,3,1,128]{3,2,1,0:T(1,128)} %bitcast.5, s32[1,1,128]{2,1,0:T(1,128)} %spec_h.1, s32[1,1,8,128]{3,2,1,0:T(8,128)} %bitcast.3, s32[1,1,8,128]{3,2,1,0:T(8,128)} %bitcast.4, s32[3,512]{1,0:T(4,128)} %wv_h.1, f32[256,256]{1,0:T(8,128)} %vw_h.1, ...), custom_call_target="tpu_custom_call" | custom-call | tf_op jit(solution)/shard_map/pallas_call | solution.py:472
  45.4 0.7 %copy.13 = f32[1,1,128,256]{3,2,1,0:T(8,128)} copy(f32[1,1,128,256]{3,2,1,0:T(8,128)S(1)} %shard_map.109) | data formatting | bytes 262144
